TPU v7x, 128 devices: a whole 4x4x4 slice. The times are simulated.
128 devices in a mesh: elem: 4 (over z), reg: 32 (over x, y, core).
Axes of the slice: x: 4, y: 4, z: 4, core: 2. Of those that a mesh axis runs over, the one named last changes fastest.
Arguments:
- rf: bfloat16 [32, 1024, 2048], P('reg', 'elem'), may hold values from -12 to 12
- tx_delay: int32 [32, 128, 512], replicated, may hold values from 1 to 1022
- rx_delay: int32 [128, 1024], P(None, 'elem'), may hold values from 0 to 1021, as said below
- aperture: int32 [128, 4], replicated, may hold values from 0 to 32, as said below
Outputs:
- image: float32 [128, 512], P('reg', 'elem')
Inputs may be any that keep to these rules, and one draw needn't show every extreme that they name: `aperture`: rows and columns are half-open ranges of the probe, each spanning 8 or more elements; some region has the whole probe. `rx_delay`: each receive delay is a delay of the region plus a delay of the element alone.
All inputs are finite; a program needn't handle non-finite values.
Results may differ from a plain program's by a relative error of at most 0.007.
Values may be sent and summed in bfloat16 or wider, within the bound.
No kernel may reach another device: no remote copies, remote signals or barrier semaphores. Data moves between devices by JAX's collectives and lax.ppermute only.
A program may use at most 448 MiB of HBM per device.

v0:
```python
import math

import jax
import jax.numpy as jnp
from jax import lax
from jax.sharding import PartitionSpec as P

PROBE = 32
SUB = 8


tap_weights = (-0.0625, 0.5625, 0.5625, -0.0625)
load_factor = 0.05


def aperture_mask(bounds, first, width):
    element = first + jnp.arange(width, dtype=jnp.int32)
    row = (element // PROBE)[None, :]
    column = (element % PROBE)[None, :]
    inside = (row >= bounds[:, 0:1]) & (row < bounds[:, 1:2])
    return inside & (column >= bounds[:, 2:3]) & (column < bounds[:, 3:4])


def delay_rows(signals, tx_part, rx_part, inside):
    count, width, samples = signals.shape
    wide = jnp.pad(signals.astype(jnp.float32), ((0, 0), (0, 0), (1, samples + 2)))
    filtered = jnp.zeros((count, width, 2 * samples), jnp.float32)
    for place, weight in enumerate(tap_weights):
        filtered = filtered + weight * wide[:, :, place : place + 2 * samples]
    filtered = filtered.astype(jnp.bfloat16)
    base = jnp.min(rx_part, axis=1)
    lead = rx_part[0]
    relative = lead - jnp.min(lead)
    shifted = jax.vmap(
        lambda trace, begin: lax.dynamic_slice_in_dim(trace, begin, samples, 1),
        in_axes=(1, 0),
        out_axes=2,
    )(filtered, relative)
    where_at = tx_part + base[None, :, None]
    picked = jax.vmap(lambda table, spots: table[spots])(shifted, where_at)
    return jnp.where(inside[None, :, None, :], picked, jnp.zeros((), jnp.bfloat16))


def block_window():
    index = jnp.arange(SUB * PROBE, dtype=jnp.int32)[:, None]
    target = jnp.arange(SUB * SUB, dtype=jnp.int32)[None, :]
    column = index % PROBE
    start = target % SUB
    same_row = index // PROBE == target // SUB
    covered = (column >= start) & (column <= start + PROBE - SUB)
    return (same_row & covered).astype(jnp.bfloat16)


def band_stats(tiles, window):
    gram = jnp.einsum("tkvi,tkvj->kij", tiles, tiles, preferred_element_type=jnp.float32)
    smooth = jnp.einsum("tkvi,iq->kqv", tiles, window, preferred_element_type=jnp.float32)
    return (gram, smooth)


def fold_cov(gram):
    regions = gram.shape[0]
    split = gram.reshape(regions, SUB, PROBE, SUB, PROBE)
    total = split[:, :, 0:SUB, :, 0:SUB]
    for shift in range(1, PROBE - SUB + 1):
        total = total + split[:, :, shift : shift + SUB, :, shift : shift + SUB]
    return total.reshape(regions, SUB * SUB, SUB * SUB)


def mvdr_weights(cov):
    regions, order, _ = cov.shape
    trace = jnp.trace(cov, axis1=1, axis2=2)
    loaded = (
        cov + (load_factor * trace / order)[:, None, None] * jnp.eye(order, dtype=jnp.float32)[None]
    )
    factor = jnp.linalg.cholesky(loaded)
    ones = jnp.ones((regions, order, 1), jnp.float32)
    middle = lax.linalg.triangular_solve(factor, ones, left_side=True, lower=True)
    solved = lax.linalg.triangular_solve(
        factor, middle, left_side=True, lower=True, transpose_a=True
    )[..., 0]
    return solved / jnp.sum(solved, axis=-1, keepdims=True)


def per_device(rf, tx_delay, rx_delay, aperture):
    n_reg = lax.axis_size("reg")
    n_elem = lax.axis_size("elem")
    tx_dev, width, samples = rf.shape
    regions, voxels = (tx_delay.shape[1], tx_delay.shape[2])
    reg_dev = regions // n_reg
    first = lax.axis_index("elem") * width
    inside = aperture_mask(aperture, first, width)
    window = block_window()
    scale = 8.0 / math.sqrt(tx_dev * n_reg * n_elem * (PROBE - SUB + 1))
    my_tx = lax.dynamic_slice_in_dim(tx_delay, lax.axis_index("reg") * tx_dev, tx_dev, 0)
    tiles = delay_rows(rf, my_tx, rx_delay, inside)
    moved = lax.all_to_all(
        tiles.reshape(tx_dev, n_reg, reg_dev, voxels * width),
        "reg",
        split_axis=1,
        concat_axis=0,
        tiled=True,
    )
    count, _, items, _ = moved.shape
    gram, part = band_stats(moved.reshape(count, items, voxels, width), window)
    cov = fold_cov(gram)
    weights = mvdr_weights(lax.psum(cov, "elem"))
    partial_image = jnp.sum(part * weights[:, :, None], axis=1) * scale
    return lax.psum_scatter(partial_image, "elem", scatter_dimension=1, tiled=True)


def solution(mesh):
    in_specs = (P("reg", "elem", None), P(), P(None, "elem"), P())
    out_specs = P("reg", "elem")
    return jax.shard_map(
        per_device, mesh=mesh, in_specs=in_specs, out_specs=out_specs, check_vma=False
    )
```

profile of v0, /device:TPU:1, one launch (start us, length us, event | category | flops | bytes accessed | tf_op | source)
XLA Modules:
  0.0 2111.4 jit_solution(13050327007082705116)
XLA Ops:
  7.5 6.1 broadcast_in_dim.25
  13.6 33.9 %broadcast_in_dim.28 = pred[1,32,4,131072]{3,2,1,0:T(4,128)(4,1)} reshape(pred[128,512,256]{2,1,0:T(8,128)(4,1)} %broadcast_in_dim.25) | data formatting | bytes 33554432 | tf_op jit(solution)/shard_map/jit(_where)/broadcast_in_dim | solution.py:41
  50.1 3.4 fusion.9
  54.3 666.9 %while.1 = (s32[]{:T(128)}, bf16[256,1,4096]{2,0,1:T(8,128)(2,1)S(1)}, s32[256,3]{0,1:T(4,128)S(1)}, bf16[256,1,2048]{2,1,0:T(2,128)(2,1)}, s32[]{:T(128)}) while((s32[]{:T(128)}, bf16[256,1,4096]{2,0,1:T(8,128)(2,1)S(1)}, s32[256,3]{0,1:T(4,128)S(1)}, bf16[256,1,2048]{2,1,0:T(2,128)(2,1)}, s32[]{:T(128)}) %tuple.28), condition=%wide.while_cond, body=%wide.while_body.sunk | while | flops 2 | bytes 13929 | solution.py:35
  60.2 1.9 bitcast_dynamic-update-slice_fusion.2
  65.4 1.9 bitcast_dynamic-update-slice_fusion.2
  70.6 1.9 bitcast_dynamic-update-slice_fusion.2
  88.8 1.9 bitcast_dynamic-update-slice_fusion.2
  94.0 1.9 bitcast_dynamic-update-slice_fusion.2
  104.4 1.9 bitcast_dynamic-update-slice_fusion.2
  112.3 1.9 bitcast_dynamic-update-slice_fusion.2
  127.9 1.9 bitcast_dynamic-update-slice_fusion.2
  133.1 1.9 bitcast_dynamic-update-slice_fusion.2
  146.1 1.9 bitcast_dynamic-update-slice_fusion.2
  151.3 1.9 bitcast_dynamic-update-slice_fusion.2
  169.6 1.9 bitcast_dynamic-update-slice_fusion.2
  193.0 1.9 bitcast_dynamic-update-slice_fusion.2
  198.2 1.9 bitcast_dynamic-update-slice_fusion.2
  224.3 1.9 bitcast_dynamic-update-slice_fusion.2
  232.1 1.9 bitcast_dynamic-update-slice_fusion.2
  245.1 1.9 bitcast_dynamic-update-slice_fusion.2
  268.5 1.9 bitcast_dynamic-update-slice_fusion.2
  281.6 1.9 bitcast_dynamic-update-slice_fusion.2
  341.5 1.9 bitcast_dynamic-update-slice_fusion.2
  362.3 1.9 bitcast_dynamic-update-slice_fusion.2
  367.5 1.9 bitcast_dynamic-update-slice_fusion.2
  372.7 1.9 bitcast_dynamic-update-slice_fusion.2
  380.6 1.9 bitcast_dynamic-update-slice_fusion.2
  398.8 1.9 bitcast_dynamic-update-slice_fusion.2
  404.0 1.9 bitcast_dynamic-update-slice_fusion.2
  411.8 1.9 bitcast_dynamic-update-slice_fusion.2
  417.0 1.9 bitcast_dynamic-update-slice_fusion.2
  419.6 1.9 bitcast_dynamic-update-slice_fusion.2
  424.9 1.9 bitcast_dynamic-update-slice_fusion.2
  430.1 1.9 bitcast_dynamic-update-slice_fusion.2
  445.7 1.9 bitcast_dynamic-update-slice_fusion.2
  453.5 1.9 bitcast_dynamic-update-slice_fusion.2
  461.3 1.9 bitcast_dynamic-update-slice_fusion.2
  490.0 1.9 bitcast_dynamic-update-slice_fusion.2
  513.4 1.9 bitcast_dynamic-update-slice_fusion.2
  529.1 1.9 bitcast_dynamic-update-slice_fusion.2
  544.7 1.9 bitcast_dynamic-update-slice_fusion.2
  589.0 1.9 bitcast_dynamic-update-slice_fusion.2
  630.6 1.9 bitcast_dynamic-update-slice_fusion.2
  648.9 1.9 bitcast_dynamic-update-slice_fusion.2
  661.9 1.9 bitcast_dynamic-update-slice_fusion.2
  675.0 1.9 bitcast_dynamic-update-slice_fusion.2
  698.4 1.9 bitcast_dynamic-update-slice_fusion.2
  716.6 1.9 bitcast_dynamic-update-slice_fusion.2
  721.2 4.5 copy.21
  725.7 558.8 %gather_fusion = bf16[65536,256]{1,0:T(8,128)(2,1)} fusion(bf16[1,2048,256]{2,1,0:T(8,128)(2,1)S(1)} %bitcast.83, s32[65536]{0:T(1024)S(1)} %bitcast.84), kind=kCustom, calls=%fused_computation | custom fusion | bytes 67633152 | tf_op jit(solution)/shard_map/vmap()/gather | solution.py:40
  1284.4 40.6 %gather.10 = bf16[1,32,4,131072]{3,2,1,0:T(4,128)(2,1)} reshape(bf16[65536,256]{1,0:T(8,128)(2,1)} %gather_fusion) | data formatting | bytes 67108864 | tf_op jit(solution)/shard_map/vmap()/gather | solution.py:40
  1325.1 29.2 %select_bitcast_fusion = bf16[1,32,4,131072]{3,2,0,1:T(4,128)(2,1)} fusion(pred[1,32,4,131072]{3,2,1,0:T(4,128)(4,1)} %broadcast_in_dim.28, bf16[1,32,4,131072]{3,2,1,0:T(4,128)(2,1)} %gather.10), kind=kLoop, calls=%fused_computation.6 | loop fusion | flops 16777216 | bytes 83886080 | tf_op jit(solution)/shard_map/jit(_where)/select_n | solution.py:41
  1354.3 8.7 all-to-all-start
  1363.2 493.8 %all-to-all-done = bf16[1,32,4,131072]{3,2,0,1:T(4,128)(2,1)} async-done(((bf16[1,32,4,131072]{3,2,0,1:T(4,128)(2,1)}), bf16[1,32,4,131072]{3,2,0,1:T(4,128)(2,1)}, u32[]{:S(2)}, u32[]{:S(2)}) %all-to-all-start) | async-done | bytes 33554464 | tf_op jit(solution)/shard_map/all_to_all | solution.py:96
  1857.0 42.6 %reshape.386 = bf16[32,4,512,256]{3,2,1,0:T(8,128)(2,1)} reshape(bf16[1,32,4,131072]{3,2,0,1:T(4,128)(2,1)} %all-to-all-done) | data formatting | bytes 67108864 | tf_op jit(solution)/shard_map/reshape | solution.py:104
  1899.7 23.8 %fusion.10 = f32[4,256,256]{2,1,0:T(8,128)S(1)} fusion(bf16[32,4,512,256]{3,2,1,0:T(8,128)(2,1)} %reshape.386), kind=kOutput, calls=%fused_computation.20 | convolution fusion | flops 8589934592 | bytes 34603008 | tf_op jit(solution)/shard_map/tkvi,tkvj->kij/dot_general | solution.py:55
  1923.4 2.5 reshape.345
  1926.0 13.9 slice_add_fusion
  1941.2 15.6 convert_reduce_fusion
  1956.8 76.6 %all-reduce.4.cloned.1.call-done = f32[4,64,64]{2,1,0:T(8,128)} async-done(((f32[4,64,64]{2,1,0:T(8,128)}), f32[4,64,64]{2,1,0:T(8,128)}) %all-reduce.4.cloned.1.call-update) | async-done | bytes 65552 | tf_op jit(solution)/shard_map/psum | solution.py:106
  2036.5 23.5 %custom-call.9 = f32[4,64,64]{2,1,0:T(8,128)S(1)} custom-call(f32[4,64,64]{2,1,0:T(8,128)S(1)} %fusion.30), custom_call_target="Cholesky" | custom-call | tf_op jit(solution)/shard_map/jit(cholesky)/cholesky | solution.py:75
  2060.2 19.7 custom-call.10
  2082.0 21.1 reduce-scatter.4.cloned.1.call-done
  (769 shorter events, 592.0 us)
Async XLA Ops:
  13.6 33.9 %copy-start.1 = (s32[128,256]{1,0:T(8,128)S(1)}, s32[128,256]{1,0:T(8,128)}, u32[]{:S(2)}) copy-start(s32[128,256]{1,0:T(8,128)} %param.6) | copy-start | bytes 393220
  13.6 36.0 %copy-start = (bf16[1,256,2048]{2,1,0:T(8,128)(2,1)S(1)}, bf16[1,256,2048]{2,1,0:T(8,128)(2,1)}, u32[]{:S(2)}) copy-start(bf16[1,256,2048]{2,1,0:T(8,128)(2,1)} %param.4) | copy-start | bytes 3145732
  1354.3 502.7 %all-to-all-start = ((bf16[1,32,4,131072]{3,2,0,1:T(4,128)(2,1)}), bf16[1,32,4,131072]{3,2,0,1:T(4,128)(2,1)}, u32[]{:S(2)}, u32[]{:S(2)}) async-start(bf16[1,32,4,131072]{3,2,0,1:T(4,128)(2,1)} %select_bitcast_fusion), calls=%async_computation | async-start | bytes 67108864 | tf_op jit(solution)/shard_map/all_to_all | solution.py:96
  1362.9 670.5 %all-reduce.4.cloned.1.call-start = ((), (), s32[]{:S(2)}) async-start(), calls=%async_computation.2 | async-start | bytes 262144 | tf_op jit(solution)/shard_map/psum | solution.py:106
  1940.9 162.2 %reduce-scatter.4.cloned.1.call-start = ((), (), s32[]{:S(2)}) async-start(), calls=%async_computation.3 | async-start | bytes 327680
Sparse Core Ops, SparseCore 0:
  1941.0 92.3 all-reduce.3
  2082.2 20.9 reduce-scatter.3
where the time goes:
time: 2120 us; the launch traced here: 2110 us
  local copies, waits for them, and re-layouts  1360 us (64%)
  waiting for transfers between devices  592 us (28%)
  other arithmetic  112 us (5%)
  matrix products  24.8 us (1%)
    gather x768, local copies, waits for them, and re-layouts  667 us
    gather x3, local copies, waits for them, and re-layouts, delay_rows(): picked = jax.vmap(lambda table, spots: table[spots])(shifted, where_at)  599 us
    all_to_all x1, waiting for transfers between devices, per_device(): lax.all_to_all(tiles.reshape(tx_dev, n_reg, reg_dev, voxels * width), 're...  494 us
    psum x1, waiting for transfers between devices, per_device(): weights = mvdr_weights(lax.psum(cov, 'elem'))  76.6 us
    reshape x1, local copies, waits for them, and re-layouts, per_device(): gram, part = band_stats(moved.reshape(count, items, voxels, width), window)  42.6 us
  transfers between devices with their start and end apart: 3, of which 3 were waited for; matrix products, arithmetic and copies ran while one was open for 1% of the time, Pallas kernels for 0%

commit v1 on v0

v1 whole, which is shorter than its diff:
```python
import functools
import math

import jax
import jax.numpy as jnp
from jax import lax
from jax.experimental import pallas as pl
from jax.experimental.pallas import tpu as pltpu
from jax.sharding import PartitionSpec as P

PROBE = 32
SUB = 8
SHIFTS = PROBE - SUB + 1
WIDTH = SUB * PROBE
ORDER = SUB * SUB
LANES = 128

tap_weights = (-0.0625, 0.5625, 0.5625, -0.0625)
load_factor = 0.05

DELTAS = (0, 1, 2, 3, 4, -4, -5, -6, -7)
TILES = 17


def lane_iota(shape):
    return lax.broadcasted_iota(jnp.int32, shape, len(shape) - 1)


def row_iota(shape):
    return lax.broadcasted_iota(jnp.int32, shape, 0)


def window_matrix(delta, half):
    element = row_iota((WIDTH, LANES))
    lane = lane_iota((WIDTH, LANES))
    target = lane - ORDER * half
    x = target & (SUB - 1)
    k = element & (PROBE - 1)
    good = (target >= 0) & (target < ORDER)
    good &= (element // PROBE) == (target // SUB)
    good &= (k >= x) & (k <= x + PROBE - SUB)
    good &= (x + delta >= 0) & (x + delta < SUB)
    return good.astype(jnp.float32).astype(jnp.bfloat16)


def split(x):
    high = x.astype(jnp.bfloat16)
    low = (x - high.astype(jnp.float32)).astype(jnp.bfloat16)
    return high, low


def stats_kernel(place, rf_ref, tx_ref, rx_ref, aperture_ref, cov_ref, traces_ref,
                 wide, shifted, count32, count16, colmask, windows):
    regions = rx_ref.shape[0]
    samples = rf_ref.shape[-1]
    blocks = samples // LANES
    voxels = tx_ref.shape[-1]
    first_row = place[1] * SUB

    rx = rx_ref[...].astype(jnp.float32)
    base = jnp.min(rx, axis=1, keepdims=True)
    lead = rx[0:1, :] - base[0:1, :]
    relative = jnp.transpose(jnp.broadcast_to(lead, (LANES, WIDTH))).astype(jnp.int32)
    wide[0:SUB, :] = jnp.zeros((SUB, samples), jnp.float32)
    wide[SUB + WIDTH : 2 * SUB + WIDTH, :] = jnp.zeros((SUB, samples), jnp.float32)
    step = 32
    for chunk in range(WIDTH // step):
        rows = slice(chunk * step, (chunk + 1) * step)
        x = rf_ref[0, rows, :].astype(jnp.float32)
        y = tap_weights[0] * pltpu.roll(x, 1, 1)
        y = y + tap_weights[1] * x
        y = y + tap_weights[2] * pltpu.roll(x, samples - 1, 1)
        y = y + tap_weights[3] * pltpu.roll(x, samples - 2, 1)
        y = y.astype(jnp.bfloat16).astype(jnp.float32)
        move = relative[rows, :]
        fine = move & (LANES - 1)
        reach = lane_iota((step, LANES)) + fine
        spot = reach & (LANES - 1)
        parts = [
            jnp.take_along_axis(y[:, j * LANES : (j + 1) * LANES], spot, axis=1)
            for j in range(blocks)
        ]
        stay = reach < LANES
        parts = [jnp.where(stay, parts[j], parts[(j + 1) % blocks]) for j in range(blocks)]
        for bit in range(3):
            here = (move & (LANES << bit)) != 0
            parts = [
                jnp.where(here, parts[(j + (1 << bit)) % blocks], parts[j]) for j in range(blocks)
            ]
        for j in range(blocks):
            wide[SUB + chunk * step : SUB + (chunk + 1) * step, j * LANES : (j + 1) * LANES] = parts[j]
    for which, delta in enumerate(DELTAS):
        for chunk in range(WIDTH // step):
            begin = SUB + chunk * step + delta
            part = wide[begin : begin + step, :].astype(jnp.bfloat16)
            shifted[which, chunk * step : (chunk + 1) * step, :] = part
            shifted[which, WIDTH + chunk * step : WIDTH + (chunk + 1) * step, :] = part
            if which == 0:
                traces_ref[chunk * step : (chunk + 1) * step, :] = part

    sums = tx_ref[0] + base.astype(jnp.int32)
    tall = 16
    high_rows = row_iota((tall, voxels))
    low_rows = row_iota((LANES, voxels))
    for r in range(regions):
        spots = sums[r : r + 1, :]
        high = jnp.where(spots // LANES == high_rows, 1.0, 0.0).astype(jnp.bfloat16)
        low = jnp.where((spots & (LANES - 1)) == low_rows, 1.0, 0.0).astype(jnp.bfloat16)
        count32[:, r, :] = lax.dot_general(
            high, low, (((1,), (1,)), ((), ())), preferred_element_type=jnp.float32
        )
    for j in range(blocks):
        count16[:, j * LANES : (j + 1) * LANES] = count32[j].astype(jnp.bfloat16)

    lane = lane_iota((regions, WIDTH))
    row = lane // PROBE
    column = lane & (PROBE - 1)
    bounds = aperture_ref[...]
    row_lo, row_hi = bounds[:, 0:1] - first_row, bounds[:, 1:2] - first_row
    col_lo, col_hi = bounds[:, 2:3], bounds[:, 3:4]
    for which, delta in enumerate(DELTAS):
        other = column + delta
        inside = (column >= col_lo) & (column < col_hi) & (other >= col_lo) & (other < col_hi)
        colmask[which] = inside.astype(jnp.float32)
    row_inside = (row >= row_lo) & (row < row_hi)

    def row_mask(da):
        other = (row + da) & (SUB - 1)
        return (row_inside & (other >= row_lo) & (other < row_hi)).astype(jnp.float32)

    for slot, (delta, half) in enumerate(
        ((1, 0), (-7, 0), (2, 1), (-6, 1), (3, 0), (-5, 0), (3, 1), (-5, 1), (4, 0), (-4, 0), (0, 1))
    ):
        windows[slot] = window_matrix(delta, half)

    def term(delta, da, rows, slot):
        which = DELTAS.index(delta)
        begin = pl.multiple_of(da * PROBE, PROBE)
        pair = shifted[0, 0:WIDTH, :] * shifted[which, pl.ds(begin, WIDTH), :]
        gram = lax.dot_general(
            count16[...], pair, (((1,), (1,)), ((), ())), preferred_element_type=jnp.float32
        )
        gram = gram * (colmask[which] * rows)
        high, low = split(gram)
        out = jnp.dot(high, windows[slot], preferred_element_type=jnp.float32)
        return out + jnp.dot(low, windows[slot], preferred_element_type=jnp.float32)

    def put(tile, value):
        cov_ref[:, pl.ds(pl.multiple_of(tile * LANES, LANES), LANES)] = value

    @pl.loop(0, SUB)
    def _(da):
        rows = row_mask(da)
        put(da, term(1, da, rows, 0) + term(-7, da, rows, 1) + term(2, da, rows, 2) + term(-6, da, rows, 3))

    @pl.loop(0, SUB // 2)
    def _(da):
        rows = row_mask(da)
        more = row_mask(da + 4)
        put(
            SUB + da,
            term(3, da, rows, 4) + term(-5, da, rows, 5) + term(3, da + 4, more, 6) + term(-5, da + 4, more, 7),
        )

    @pl.loop(0, SUB // 2 + 1)
    def _(da):
        rows = row_mask(da)
        put(12 + da, term(4, da, rows, 8) + term(-4, da, rows, 9) + term(0, da, rows, 10))


def stats(place, rf, tx_delay, rx_delay, aperture):
    regions = rx_delay.shape[0]
    samples = rf.shape[-1]
    voxels = tx_delay.shape[-1]
    grid_spec = pltpu.PrefetchScalarGridSpec(
        num_scalar_prefetch=1,
        grid=(1,),
        in_specs=[
            pl.BlockSpec(rf.shape, lambda i, place: (0, 0, 0)),
            pl.BlockSpec((1, regions, voxels), lambda i, place: (place[0], 0, 0)),
            pl.BlockSpec(rx_delay.shape, lambda i, place: (0, 0)),
            pl.BlockSpec(aperture.shape, lambda i, place: (0, 0)),
        ],
        out_specs=[
            pl.BlockSpec((regions, TILES * LANES), lambda i, place: (0, 0)),
            pl.BlockSpec((WIDTH, samples), lambda i, place: (0, 0)),
        ],
        scratch_shapes=[
            pltpu.VMEM((WIDTH + 2 * SUB, samples), jnp.float32),
            pltpu.VMEM((len(DELTAS), 2 * WIDTH, samples), jnp.bfloat16),
            pltpu.VMEM((16, regions, LANES), jnp.float32),
            pltpu.VMEM((regions, samples), jnp.bfloat16),
            pltpu.VMEM((len(DELTAS), regions, WIDTH), jnp.float32),
            pltpu.VMEM((11, WIDTH, LANES), jnp.bfloat16),
        ],
    )
    return pl.pallas_call(
        stats_kernel,
        grid_spec=grid_spec,
        out_shape=[
            jax.ShapeDtypeStruct((regions, TILES * LANES), jnp.float32),
            jax.ShapeDtypeStruct((WIDTH, samples), jnp.bfloat16),
        ],
        compiler_params=pltpu.CompilerParams(vmem_limit_bytes=56 * 1024 * 1024),
        name="stats",
    )(place, rf, tx_delay, rx_delay, aperture)


def solve_kernel(parts_ref, weights_ref):
    total = jnp.sum(parts_ref[...], axis=0, keepdims=True)
    tiles = [total[:, t * LANES : (t + 1) * LANES] for t in range(TILES)]
    tall = jnp.concatenate(tiles + [jnp.zeros((LANES - TILES, LANES), jnp.float32)], axis=0)
    turned = jnp.transpose(tall)
    table = jnp.concatenate([turned[0:ORDER, 0:ORDER], turned[ORDER:LANES, 0:ORDER]], axis=1)
    i = row_iota((ORDER, LANES))
    lane = lane_iota((ORDER, LANES))
    j = lane & (ORDER - 1)
    da = ((j // SUB) - (i // SUB)) & (SUB - 1)
    d = ((j & (SUB - 1)) - (i & (SUB - 1))) & (SUB - 1)
    spot = jnp.where(
        d == 1, da,
        jnp.where(
            d == 2, da + ORDER,
            jnp.where(
                d == 3, SUB + (da & 3) + ORDER * (da // 4),
                jnp.where(d == 4, 12 + da, 12 + da + ORDER),
            ),
        ),
    )
    stored = ((d >= 1) & (d <= 3)) | (((d == 0) | (d == 4)) & (da <= 4))
    half = jnp.take_along_axis(table, spot & (LANES - 1), axis=1)
    half = jnp.where(stored & (lane < ORDER), half, 0.0)
    square = jnp.concatenate([half, jnp.zeros((LANES - ORDER, LANES), jnp.float32)], axis=0)
    cov = jnp.where(stored, half, jnp.transpose(square)[0:ORDER, :])
    diagonal = lane == i
    trace = jnp.sum(jnp.sum(jnp.where(diagonal, cov, 0.0), axis=1, keepdims=True), axis=0, keepdims=True)
    cov = cov + jnp.where(diagonal, load_factor * trace / ORDER, 0.0)
    work = jnp.where(lane < ORDER, cov, 1.0)
    column = i[:, 0:1]
    for k in range(ORDER):
        pivot_row = work[k : k + 1, :]
        inverse = 1.0 / pivot_row[:, k : k + 1]
        factor = jnp.where(column == k, 0.0, work[:, k : k + 1] * inverse)
        work = work - factor * pivot_row
    held = jnp.sum(jnp.where(diagonal, work, 0.0), axis=1, keepdims=True)
    solved = work[:, ORDER : ORDER + 1] / held
    row = jnp.sum(jnp.where(diagonal, solved, 0.0), axis=0, keepdims=True)
    weights_ref[...] = row / jnp.sum(row, axis=1, keepdims=True)


def solve(parts):
    return pl.pallas_call(
        solve_kernel,
        out_shape=jax.ShapeDtypeStruct((1, LANES), jnp.float32),
        compiler_params=pltpu.CompilerParams(vmem_limit_bytes=32 * 1024 * 1024),
        name="solve",
    )(parts)


def image_kernel(place, weights_ref, traces_ref, tx_ref, rx_ref, aperture_ref, out_ref, line_ref):
    regions = rx_ref.shape[0]
    samples = traces_ref.shape[-1]
    voxels = tx_ref.shape[-1]
    first_row = place[1] * SUB

    source = row_iota((LANES, WIDTH))
    element = lane_iota((LANES, WIDTH))
    x = source & (SUB - 1)
    k = element & (PROBE - 1)
    spread = (source // SUB == element // PROBE) & (k >= x) & (k <= x + PROBE - SUB)
    spread = spread.astype(jnp.float32).astype(jnp.bfloat16)
    weights = weights_ref[...]
    high, low = split(weights)
    rest = (weights - high.astype(jnp.float32) - low.astype(jnp.float32)).astype(jnp.bfloat16)
    gain = jnp.dot(high, spread, preferred_element_type=jnp.float32)
    gain = gain + jnp.dot(low, spread, preferred_element_type=jnp.float32)
    gain = gain + jnp.dot(rest, spread, preferred_element_type=jnp.float32)
    lane = lane_iota((regions, WIDTH))
    row = lane // PROBE + first_row
    column = lane & (PROBE - 1)
    bounds = aperture_ref[...]
    inside = (row >= bounds[:, 0:1]) & (row < bounds[:, 1:2])
    inside &= (column >= bounds[:, 2:3]) & (column < bounds[:, 3:4])
    high, low = split(jnp.where(inside, gain, 0.0))
    line_ref[...] = jnp.dot(high, traces_ref[...], preferred_element_type=jnp.float32) + jnp.dot(
        low, traces_ref[...], preferred_element_type=jnp.float32
    )

    base = jnp.min(rx_ref[...].astype(jnp.float32), axis=1, keepdims=True).astype(jnp.int32)
    sums = tx_ref[0] + base
    group = 32
    for begin in range(0, regions, group):
        rows = slice(begin, begin + group)
        for v in range(voxels // LANES):
            spots = sums[rows, v * LANES : (v + 1) * LANES]
            fine = spots & (LANES - 1)
            coarse = spots // LANES
            picked = jnp.zeros((group, LANES), jnp.float32)
            for j in range(samples // LANES):
                found = jnp.take_along_axis(line_ref[rows, j * LANES : (j + 1) * LANES], fine, axis=1)
                picked = jnp.where(coarse == j, found, picked)
            out_ref[rows, v * LANES : (v + 1) * LANES] = picked


def image(place, weights, traces, tx_delay, rx_delay, aperture):
    regions = rx_delay.shape[0]
    samples = traces.shape[-1]
    voxels = tx_delay.shape[-1]
    grid_spec = pltpu.PrefetchScalarGridSpec(
        num_scalar_prefetch=1,
        grid=(1,),
        in_specs=[
            pl.BlockSpec(weights.shape, lambda i, place: (0, 0)),
            pl.BlockSpec(traces.shape, lambda i, place: (0, 0)),
            pl.BlockSpec((1, regions, voxels), lambda i, place: (place[0], 0, 0)),
            pl.BlockSpec(rx_delay.shape, lambda i, place: (0, 0)),
            pl.BlockSpec(aperture.shape, lambda i, place: (0, 0)),
        ],
        out_specs=pl.BlockSpec((regions, voxels), lambda i, place: (0, 0)),
        scratch_shapes=[pltpu.VMEM((regions, samples), jnp.float32)],
    )
    return pl.pallas_call(
        image_kernel,
        grid_spec=grid_spec,
        out_shape=jax.ShapeDtypeStruct((regions, voxels), jnp.float32),
        compiler_params=pltpu.CompilerParams(vmem_limit_bytes=32 * 1024 * 1024),
        name="image",
    )(place, weights, traces, tx_delay, rx_delay, aperture)


BOTH = ("reg", "elem")


def per_device(rf, tx_delay, rx_delay, aperture):
    n_reg = lax.axis_size("reg")
    n_elem = lax.axis_size("elem")
    regions, voxels = rx_delay.shape[0], tx_delay.shape[2]
    devices = n_reg * n_elem
    scale = 8.0 / math.sqrt(n_reg * n_elem * SHIFTS)
    place = jnp.stack([lax.axis_index("reg"), lax.axis_index("elem")]).astype(jnp.int32)
    cov, traces = stats(place, rf, tx_delay, rx_delay, aperture)
    parts = lax.all_to_all(cov, BOTH, 0, 0, tiled=True)
    mine = solve(parts)
    weights = lax.all_to_all(jnp.broadcast_to(mine, (devices, LANES)), BOTH, 0, 0, tiled=True)
    partial = image(place, weights, traces, tx_delay, rx_delay, aperture)
    owned = partial.reshape(n_reg, regions // n_reg, n_elem, voxels // n_elem).transpose(0, 2, 1, 3)
    owned = owned.reshape(devices, regions // n_reg, voxels // n_elem)
    arrived = lax.all_to_all(owned, BOTH, 0, 0, tiled=True)
    return jnp.sum(arrived, axis=0) * scale


def solution(mesh):
    in_specs = (P("reg", "elem", None), P(), P(None, "elem"), P())
    out_specs = P("reg", "elem")
    return jax.shard_map(
        per_device, mesh=mesh, in_specs=in_specs, out_specs=out_specs, check_vma=False
    )
```

time: 2120 us -> 136 us (0.06)
  local copies, waits for them, and re-layouts: 1360 us -> 7.63 us
  waiting for transfers between devices: 592 us -> 0 us
  other arithmetic: 112 us -> 1.38 us
  Pallas kernels: 0 us -> 66.4 us
  blocking collectives: 0 us -> 60.2 us
  matrix products: 24.8 us -> 0 us
    gather x772 -> x0, local copies, waits for them, and re-layouts: 1270 us -> none
    all_to_all x1 -> x0, waiting for transfers between devices: 494 us -> none  [per_device(): lax.all_to_all(tiles.reshape(tx_dev, n_reg, reg_dev, voxels * width), 're...]
    psum x1 -> x0, waiting for transfers between devices: 76.6 us -> none  [per_device(): weights = mvdr_weights(lax.psum(cov, 'elem'))]
    pallas_call x0 -> x3, Pallas kernels: none -> 66.4 us  [the longest x1 56.3 us: stats(): pl.pallas_call(stats_kernel, grid_spec=grid_spec, out_shape=[jax.ShapeDty...]
    all_to_all x0 -> x3, blocking collectives: none -> 60.2 us  [the longest x1 31.6 us: per_device(): parts = lax.all_to_all(cov, BOTH, 0, 0, tiled=True)]
    reshape x3, local copies, waits for them, and re-layouts: 46.1 us -> 0.32 us  [the longest x1 0.17 us: per_device(): owned = owned.reshape(devices, regions // n_reg, voxels // n_elem)]
    another operation x7 -> x1, other arithmetic: 43.4 us -> 0.65 us  [per_device(): jnp.stack([lax.axis_index('reg'), lax.axis_index('elem')]).astype(jnp.int32)]
    broadcast_in_dim x2 -> x1, local copies, waits for them, and re-layouts: 40 us -> 0.05 us  [per_device(): jnp.broadcast_to(mine, (devices, LANES))]
  transfers between devices with their start and end apart: 3 -> 0, of which waited for: 3 -> 0; matrix products, arithmetic and copies ran while one was open for 1% -> 0% of each run, Pallas kernels for 0% -> 0%
where the time goes in v1:
time: 136 us
  Pallas kernels  66.4 us (49%)
  blocking collectives  60.2 us (44%)
  local copies, waits for them, and re-layouts  7.63 us (6%)
  other arithmetic  1.38 us (1%)
    pallas_call x1, Pallas kernels, stats(): pl.pallas_call(stats_kernel, grid_spec=grid_spec, out_shape=[jax.ShapeDty...  56.3 us
    all_to_all x1, blocking collectives, per_device(): parts = lax.all_to_all(cov, BOTH, 0, 0, tiled=True)  31.6 us
    all_to_all x1, blocking collectives, per_device(): arrived = lax.all_to_all(owned, BOTH, 0, 0, tiled=True)  15.2 us
    all_to_all x1, blocking collectives, per_device(): lax.all_to_all(jnp.broadcast_to(mine, (devices, LANES)), BOTH, 0, 0, tile...  13.3 us
    pallas_call x1, Pallas kernels, solve(): pl.pallas_call(solve_kernel, out_shape=jax.ShapeDtypeStruct((1, LANES), j...  6.07 us
    unnamed x12, local copies, waits for them, and re-layouts  4.87 us
    pallas_call x1, Pallas kernels, image(): pl.pallas_call(image_kernel, grid_spec=grid_spec, out_shape=jax.ShapeDtyp...  3.97 us

profile of v1, /device:TPU:1, one launch (start us, length us, event | category | flops | bytes accessed | tf_op | source)
XLA Modules:
  0.0 135.7 jit_solution(7537921158522135332)
XLA Ops:
  0.0 1.4 %copy.10.aperture_ref = s32[128,4]{1,0:T(8,128)} copy(s32[128,4]{0,1:T(4,128)} %param.7) | data formatting | bytes 4096 | tf_op args[3]
  1.4 0.7 pad_add_fusion.place
  2.1 56.3 %stats.1 = (f32[128,2176]{1,0:T(8,128)}, bf16[256,2048]{1,0:T(8,128)(2,1)}) custom-call(s32[2]{0:T(128)} %pad_add_fusion.place, bf16[1,256,2048]{2,1,0:T(8,128)(2,1)} %rf_ref.1, s32[32,128,512]{2,1,0:T(8,128)} %tx_ref.3, s32[128,256]{1,0:T(8,128)} %rx_ref.3, s32[128,4]{1,0:T(8,128)} %copy.10.aperture_ref), custom_call_target="tpu_custom_call" | custom-call | tf_op jit(solution)/shard_map/stats/pallas_call | solution.py:197
  58.4 2.4 %copy.11 = f32[128,1,2176]{2,1,0:T(1,128)S(1)} copy(f32[128,1,2176]{2,0,1:T(8,128)} %bitcast.14) | data formatting | bytes 2228224 | tf_op jit(solution)/shard_map/all_to_all | solution.py:342
  60.8 31.6 %all_to_all.24 = f32[128,1,2176]{2,1,0:T(1,128)S(1)} all-to-all(f32[128,1,2176]{2,1,0:T(1,128)S(1)} %copy.11), channel_id=1, replica_groups=mesh['elem'=4,'reg'=32] {'reg','elem'}, dimensions={0} | all-to-all | bytes 2228224 | tf_op jit(solution)/shard_map/all_to_all | solution.py:342
  92.4 0.1 copy.17
  92.5 0.0 copy-start.1
  92.5 0.0 copy-start.2
  92.5 0.0 copy-start.3
  92.5 0.0 copy-start.4
  92.5 6.1 %solve.1 = f32[1,128]{1,0:T(1,128)S(1)} custom-call(f32[128,2176]{1,0:T(8,128)S(1)} %bitcast.11), custom_call_target="tpu_custom_call" | custom-call | tf_op jit(solution)/shard_map/solve/pallas_call | solution.py:252
  98.6 13.3 %all_to_all.25 = f32[128,1,128]{2,1,0:T(1,128)S(1)} all-to-all(f32[128,1,128]{2,1,0:T(1,128)S(1)} %broadcast_in_dim.2), channel_id=1, replica_groups=mesh['elem'=4,'reg'=32] {'reg','elem'}, dimensions={0} | all-to-all | bytes 131072 | tf_op jit(solution)/shard_map/all_to_all | solution.py:344
  112.0 0.0 copy-done.1
  112.0 0.0 copy-done.2
  112.0 0.0 copy-done.3
  112.0 0.0 copy-done.4
  112.0 0.0 copy-start
  112.0 3.4 %copy-done = s32[32,128,512]{2,1,0:T(8,128)S(1)} copy-done((s32[32,128,512]{2,1,0:T(8,128)S(1)}, s32[32,128,512]{2,1,0:T(8,128)}, u32[]{:S(2)}) %copy-start) | copy-done | bytes 8388632
  115.4 4.0 %image.1 = f32[128,512]{1,0:T(8,128)S(1)} custom-call(s32[2]{0:T(128)S(1)} %copy-done.4, f32[128,128]{1,0:T(8,128)S(1)} %bitcast.12, bf16[256,2048]{1,0:T(8,128)(2,1)S(1)} %copy-done.1, s32[32,128,512]{2,1,0:T(8,128)S(1)} %copy-done, s32[128,256]{1,0:T(8,128)S(1)} %copy-done.3, s32[128,4]{1,0:T(8,128)S(1)} %copy-done.2), custom_call_target="tpu_custom_call" | custom-call | tf_op jit(solution)/shard_map/image/pallas_call | solution.py:322
  119.4 0.1 reshape.14
  119.5 0.2 copy.14
  119.7 15.2 %all_to_all.26 = f32[128,4,128]{2,1,0:T(4,128)S(1)} all-to-all(f32[128,4,128]{2,1,0:T(4,128)S(1)} %copy.14), channel_id=1, replica_groups=mesh['elem'=4,'reg'=32] {'reg','elem'}, dimensions={0} | all-to-all | bytes 524288 | tf_op jit(solution)/shard_map/all_to_all | solution.py:348
  134.9 0.1 reduce_sum.9
  135.1 0.6 broadcast_multiply_fusion
  (2 shorter events, 0.1 us)
Async XLA Ops:
  92.5 19.5 %copy-start.1 = (bf16[256,2048]{1,0:T(8,128)(2,1)S(1)}, bf16[256,2048]{1,0:T(8,128)(2,1)}, u32[]{:S(2)}) copy-start(bf16[256,2048]{1,0:T(8,128)(2,1)} %get-tuple-element.8.traces_ref) | copy-start | bytes 3145732
  92.5 19.5 %copy-start.2 = (s32[128,4]{1,0:T(8,128)S(1)}, s32[128,4]{1,0:T(8,128)}, u32[]{:S(2)}) copy-start(s32[128,4]{1,0:T(8,128)} %copy.10.aperture_ref) | copy-start | bytes 6148
  92.5 19.5 %copy-start.3 = (s32[128,256]{1,0:T(8,128)S(1)}, s32[128,256]{1,0:T(8,128)}, u32[]{:S(2)}) copy-start(s32[128,256]{1,0:T(8,128)} %rx_ref.3) | copy-start | bytes 393220
  92.5 19.5 %copy-start.4 = (s32[2]{0:T(128)S(1)}, s32[2]{0:T(128)}, u32[]{:S(2)}) copy-start(s32[2]{0:T(128)} %pad_add_fusion.place) | copy-start | bytes 28
  112.0 3.4 %copy-start = (s32[32,128,512]{2,1,0:T(8,128)S(1)}, s32[32,128,512]{2,1,0:T(8,128)}, u32[]{:S(2)}) copy-start(s32[32,128,512]{2,1,0:T(8,128)} %tx_ref.3) | copy-start | bytes 25165828

commit v2 on v1

--- a/solution.py
+++ b/solution.py
@@ -20,6 +20,7 @@
 
 DELTAS = (0, 1, 2, 3, 4, -4, -5, -6, -7)
 TILES = 17
+WINDOWS = ((1, 0), (-7, 0), (2, 1), (-6, 1), (3, 0), (-5, 0), (3, 1), (-5, 1), (4, 0), (-4, 0), (0, 1))
 
 
 def lane_iota(shape):
@@ -31,9 +32,8 @@
 
 
 def window_matrix(delta, half):
-    element = row_iota((WIDTH, LANES))
-    lane = lane_iota((WIDTH, LANES))
-    target = lane - ORDER * half
+    element = lane_iota((LANES, WIDTH))
+    target = row_iota((LANES, WIDTH)) - ORDER * half
     x = target & (SUB - 1)
     k = element & (PROBE - 1)
     good = (target >= 0) & (target < ORDER)
@@ -49,13 +49,14 @@
     return high, low
 
 
-def stats_kernel(place, rf_ref, tx_ref, rx_ref, aperture_ref, cov_ref, traces_ref,
-                 wide, shifted, count32, count16, colmask, windows):
+def stats_kernel(elem, reg, rf_ref, tx_ref, rx_ref, aperture_ref, cov_ref, traces_ref, spots_ref,
+                 wide, shifted, count32, count16, colmask, rowmask, windows, grams):
+    del reg
     regions = rx_ref.shape[0]
     samples = rf_ref.shape[-1]
     blocks = samples // LANES
     voxels = tx_ref.shape[-1]
-    first_row = place[1] * SUB
+    first_row = elem[0] * SUB
 
     rx = rx_ref[...].astype(jnp.float32)
     base = jnp.min(rx, axis=1, keepdims=True)
@@ -89,16 +90,25 @@
             ]
         for j in range(blocks):
             wide[SUB + chunk * step : SUB + (chunk + 1) * step, j * LANES : (j + 1) * LANES] = parts[j]
-    for which, delta in enumerate(DELTAS):
-        for chunk in range(WIDTH // step):
-            begin = SUB + chunk * step + delta
-            part = wide[begin : begin + step, :].astype(jnp.bfloat16)
-            shifted[which, chunk * step : (chunk + 1) * step, :] = part
-            shifted[which, WIDTH + chunk * step : WIDTH + (chunk + 1) * step, :] = part
-            if which == 0:
-                traces_ref[chunk * step : (chunk + 1) * step, :] = part
+
+    def shift_rows(which, chunk):
+        begin = SUB + DELTAS[which]
+        if isinstance(chunk, int):
+            part = wide[begin + chunk * step : begin + (chunk + 1) * step, :]
+        else:
+            around = wide[pl.ds(pl.multiple_of(chunk * step, step), step + 2 * SUB), :]
+            part = around[begin : begin + step]
+        part = part.astype(jnp.bfloat16)
+        for copy in range(2):
+            shifted[which, pl.ds(pl.multiple_of(copy * WIDTH + chunk * step, step), step), :] = part
+        return part
+
+    for chunk in range(WIDTH // step):
+        traces_ref[chunk * step : (chunk + 1) * step, :] = shift_rows(0, chunk)
+        shift_rows(1, chunk)
 
     sums = tx_ref[0] + base.astype(jnp.int32)
+    spots_ref[...] = sums
     tall = 16
     high_rows = row_iota((tall, voxels))
     low_rows = row_iota((LANES, voxels))
@@ -110,104 +120,101 @@
             high, low, (((1,), (1,)), ((), ())), preferred_element_type=jnp.float32
         )
     for j in range(blocks):
-        count16[:, j * LANES : (j + 1) * LANES] = count32[j].astype(jnp.bfloat16)
-
-    lane = lane_iota((regions, WIDTH))
-    row = lane // PROBE
-    column = lane & (PROBE - 1)
+        count16[j * LANES : (j + 1) * LANES, :] = jnp.transpose(count32[j]).astype(jnp.bfloat16)
+
+    element = row_iota((WIDTH, regions))
+    row = element // PROBE
+    column = element & (PROBE - 1)
     bounds = aperture_ref[...]
-    row_lo, row_hi = bounds[:, 0:1] - first_row, bounds[:, 1:2] - first_row
-    col_lo, col_hi = bounds[:, 2:3], bounds[:, 3:4]
+    row_lo, row_hi = bounds[0:1, :] - first_row, bounds[1:2, :] - first_row
+    col_lo, col_hi = bounds[2:3, :], bounds[3:4, :]
+    column_inside = (column >= col_lo) & (column < col_hi)
     for which, delta in enumerate(DELTAS):
         other = column + delta
-        inside = (column >= col_lo) & (column < col_hi) & (other >= col_lo) & (other < col_hi)
-        colmask[which] = inside.astype(jnp.float32)
+        inside = column_inside & (other >= col_lo) & (other < col_hi)
+        colmask[which] = inside.astype(jnp.float32).astype(jnp.bfloat16)
     row_inside = (row >= row_lo) & (row < row_hi)
-
-    def row_mask(da):
+    for da in range(SUB):
         other = (row + da) & (SUB - 1)
-        return (row_inside & (other >= row_lo) & (other < row_hi)).astype(jnp.float32)
-
-    for slot, (delta, half) in enumerate(
-        ((1, 0), (-7, 0), (2, 1), (-6, 1), (3, 0), (-5, 0), (3, 1), (-5, 1), (4, 0), (-4, 0), (0, 1))
-    ):
+        inside = row_inside & (other >= row_lo) & (other < row_hi)
+        rowmask[da] = inside.astype(jnp.float32).astype(jnp.bfloat16)
+
+    for slot, (delta, half) in enumerate(WINDOWS):
         windows[slot] = window_matrix(delta, half)
 
-    def term(delta, da, rows, slot):
-        which = DELTAS.index(delta)
-        begin = pl.multiple_of(da * PROBE, PROBE)
-        pair = shifted[0, 0:WIDTH, :] * shifted[which, pl.ds(begin, WIDTH), :]
-        gram = lax.dot_general(
-            count16[...], pair, (((1,), (1,)), ((), ())), preferred_element_type=jnp.float32
-        )
-        gram = gram * (colmask[which] * rows)
-        high, low = split(gram)
-        out = jnp.dot(high, windows[slot], preferred_element_type=jnp.float32)
-        return out + jnp.dot(low, windows[slot], preferred_element_type=jnp.float32)
-
-    def put(tile, value):
-        cov_ref[:, pl.ds(pl.multiple_of(tile * LANES, LANES), LANES)] = value
-
-    @pl.loop(0, SUB)
-    def _(da):
-        rows = row_mask(da)
-        put(da, term(1, da, rows, 0) + term(-7, da, rows, 1) + term(2, da, rows, 2) + term(-6, da, rows, 3))
-
-    @pl.loop(0, SUB // 2)
-    def _(da):
-        rows = row_mask(da)
-        more = row_mask(da + 4)
-        put(
-            SUB + da,
-            term(3, da, rows, 4) + term(-5, da, rows, 5) + term(3, da + 4, more, 6) + term(-5, da + 4, more, 7),
-        )
-
-    @pl.loop(0, SUB // 2 + 1)
-    def _(da):
-        rows = row_mask(da)
-        put(12 + da, term(4, da, rows, 8) + term(-4, da, rows, 9) + term(0, da, rows, 10))
-
-
-def stats(place, rf, tx_delay, rx_delay, aperture):
+    for which, delta in enumerate(DELTAS):
+        reach = SUB if delta in (1, 2, 3, -5, -6, -7) else SUB // 2 + 1
+        if 1 <= which < len(DELTAS) - 1:
+            for chunk in range(WIDTH // step):
+                shift_rows(which + 1, chunk)
+        lead_rows = shifted[0, 0:WIDTH, :]
+        pairs = [
+            lead_rows * shifted[which, da * PROBE : da * PROBE + WIDTH, :] for da in range(reach)
+        ]
+        gram = jnp.dot(
+            jnp.concatenate(pairs, axis=0), count16[...], preferred_element_type=jnp.float32
+        ).astype(jnp.bfloat16)
+        for da in range(reach):
+            grams[which, da] = gram[da * WIDTH : (da + 1) * WIDTH] * colmask[which] * rowmask[da]
+
+    def put(tile, terms):
+        left = jnp.concatenate([windows[WINDOWS.index((delta, half))] for delta, half, da in terms], axis=1)
+        right = jnp.concatenate([grams[DELTAS.index(delta), da] for delta, half, da in terms], axis=0)
+        out = jnp.dot(left, right, preferred_element_type=jnp.float32)
+        cov_ref[:, tile * LANES : (tile + 1) * LANES] = jnp.transpose(out).astype(cov_ref.dtype)
+
+    for da in range(SUB):
+        put(da, ((1, 0, da), (-7, 0, da), (2, 1, da), (-6, 1, da)))
+    for da in range(SUB // 2):
+        put(SUB + da, ((3, 0, da), (-5, 0, da), (3, 1, da + 4), (-5, 1, da + 4)))
+    for da in range(SUB // 2 + 1):
+        put(12 + da, ((4, 0, da), (-4, 0, da), (0, 1, da)))
+
+
+def stats(elem, reg, rf, tx_delay, rx_delay, aperture):
     regions = rx_delay.shape[0]
     samples = rf.shape[-1]
     voxels = tx_delay.shape[-1]
     grid_spec = pltpu.PrefetchScalarGridSpec(
-        num_scalar_prefetch=1,
+        num_scalar_prefetch=2,
         grid=(1,),
         in_specs=[
-            pl.BlockSpec(rf.shape, lambda i, place: (0, 0, 0)),
-            pl.BlockSpec((1, regions, voxels), lambda i, place: (place[0], 0, 0)),
-            pl.BlockSpec(rx_delay.shape, lambda i, place: (0, 0)),
-            pl.BlockSpec(aperture.shape, lambda i, place: (0, 0)),
+            pl.BlockSpec(rf.shape, lambda i, elem, reg: (0, 0, 0)),
+            pl.BlockSpec((1, regions, voxels), lambda i, elem, reg: (reg[0], 0, 0)),
+            pl.BlockSpec(rx_delay.shape, lambda i, elem, reg: (0, 0)),
+            pl.BlockSpec(aperture.shape, lambda i, elem, reg: (0, 0)),
         ],
         out_specs=[
-            pl.BlockSpec((regions, TILES * LANES), lambda i, place: (0, 0)),
-            pl.BlockSpec((WIDTH, samples), lambda i, place: (0, 0)),
+            pl.BlockSpec((regions, TILES * LANES), lambda i, elem, reg: (0, 0)),
+            pl.BlockSpec((WIDTH, samples), lambda i, elem, reg: (0, 0)),
+            pl.BlockSpec((regions, voxels), lambda i, elem, reg: (0, 0)),
         ],
         scratch_shapes=[
             pltpu.VMEM((WIDTH + 2 * SUB, samples), jnp.float32),
             pltpu.VMEM((len(DELTAS), 2 * WIDTH, samples), jnp.bfloat16),
             pltpu.VMEM((16, regions, LANES), jnp.float32),
-            pltpu.VMEM((regions, samples), jnp.bfloat16),
-            pltpu.VMEM((len(DELTAS), regions, WIDTH), jnp.float32),
-            pltpu.VMEM((11, WIDTH, LANES), jnp.bfloat16),
+            pltpu.VMEM((samples, regions), jnp.bfloat16),
+            pltpu.VMEM((len(DELTAS), WIDTH, regions), jnp.bfloat16),
+            pltpu.VMEM((SUB, WIDTH, regions), jnp.bfloat16),
+            pltpu.VMEM((len(WINDOWS), LANES, WIDTH), jnp.bfloat16),
+            pltpu.VMEM((len(DELTAS), SUB, WIDTH, regions), jnp.bfloat16),
         ],
     )
     return pl.pallas_call(
         stats_kernel,
         grid_spec=grid_spec,
         out_shape=[
-            jax.ShapeDtypeStruct((regions, TILES * LANES), jnp.float32),
+            jax.ShapeDtypeStruct((regions, TILES * LANES), jnp.bfloat16),
             jax.ShapeDtypeStruct((WIDTH, samples), jnp.bfloat16),
+            jax.ShapeDtypeStruct((regions, voxels), jnp.int32),
         ],
         compiler_params=pltpu.CompilerParams(vmem_limit_bytes=56 * 1024 * 1024),
         name="stats",
-    )(place, rf, tx_delay, rx_delay, aperture)
+    )(elem, reg, rf, tx_delay, rx_delay, aperture)
 
 
 def solve_kernel(parts_ref, weights_ref):
-    total = jnp.sum(parts_ref[...], axis=0, keepdims=True)
+    total = jnp.sum(parts_ref[...].astype(jnp.float32), axis=0, keepdims=True)
     tiles = [total[:, t * LANES : (t + 1) * LANES] for t in range(TILES)]
     tall = jnp.concatenate(tiles + [jnp.zeros((LANES - TILES, LANES), jnp.float32)], axis=0)
     turned = jnp.transpose(tall)
@@ -257,11 +264,10 @@
     )(parts)
 
 
-def image_kernel(place, weights_ref, traces_ref, tx_ref, rx_ref, aperture_ref, out_ref, line_ref):
-    regions = rx_ref.shape[0]
+def image_kernel(scale, elem, weights_ref, traces_ref, spots_ref, aperture_ref, out_ref, line_ref):
+    regions, voxels = spots_ref.shape
     samples = traces_ref.shape[-1]
-    voxels = tx_ref.shape[-1]
-    first_row = place[1] * SUB
+    first_row = elem[0] * SUB
 
     source = row_iota((LANES, WIDTH))
     element = lane_iota((LANES, WIDTH))
@@ -278,16 +284,17 @@
     lane = lane_iota((regions, WIDTH))
     row = lane // PROBE + first_row
     column = lane & (PROBE - 1)
-    bounds = aperture_ref[...]
+    bounds = aperture_ref[...].astype(jnp.float32)
+    bounds = jnp.concatenate([bounds, jnp.zeros((LANES - 4, regions), jnp.float32)], axis=0)
+    bounds = jnp.transpose(bounds).astype(jnp.int32)
     inside = (row >= bounds[:, 0:1]) & (row < bounds[:, 1:2])
     inside &= (column >= bounds[:, 2:3]) & (column < bounds[:, 3:4])
-    high, low = split(jnp.where(inside, gain, 0.0))
+    high, low = split(jnp.where(inside, gain * scale, 0.0))
     line_ref[...] = jnp.dot(high, traces_ref[...], preferred_element_type=jnp.float32) + jnp.dot(
         low, traces_ref[...], preferred_element_type=jnp.float32
     )
 
-    base = jnp.min(rx_ref[...].astype(jnp.float32), axis=1, keepdims=True).astype(jnp.int32)
-    sums = tx_ref[0] + base
+    sums = spots_ref[...]
     group = 32
     for begin in range(0, regions, group):
         rows = slice(begin, begin + group)
@@ -302,30 +309,28 @@
             out_ref[rows, v * LANES : (v + 1) * LANES] = picked
 
 
-def image(place, weights, traces, tx_delay, rx_delay, aperture):
-    regions = rx_delay.shape[0]
+def image(scale, elem, weights, traces, spots, aperture):
+    regions, voxels = spots.shape
     samples = traces.shape[-1]
-    voxels = tx_delay.shape[-1]
     grid_spec = pltpu.PrefetchScalarGridSpec(
         num_scalar_prefetch=1,
         grid=(1,),
         in_specs=[
-            pl.BlockSpec(weights.shape, lambda i, place: (0, 0)),
-            pl.BlockSpec(traces.shape, lambda i, place: (0, 0)),
-            pl.BlockSpec((1, regions, voxels), lambda i, place: (place[0], 0, 0)),
-            pl.BlockSpec(rx_delay.shape, lambda i, place: (0, 0)),
-            pl.BlockSpec(aperture.shape, lambda i, place: (0, 0)),
-        ],
-        out_specs=pl.BlockSpec((regions, voxels), lambda i, place: (0, 0)),
+            pl.BlockSpec(weights.shape, lambda i, elem: (0, 0)),
+            pl.BlockSpec(traces.shape, lambda i, elem: (0, 0)),
+            pl.BlockSpec(spots.shape, lambda i, elem: (0, 0)),
+            pl.BlockSpec(aperture.shape, lambda i, elem: (0, 0)),
+        ],
+        out_specs=pl.BlockSpec((regions, voxels), lambda i, elem: (0, 0)),
         scratch_shapes=[pltpu.VMEM((regions, samples), jnp.float32)],
     )
     return pl.pallas_call(
-        image_kernel,
+        functools.partial(image_kernel, scale),
         grid_spec=grid_spec,
         out_shape=jax.ShapeDtypeStruct((regions, voxels), jnp.float32),
         compiler_params=pltpu.CompilerParams(vmem_limit_bytes=32 * 1024 * 1024),
         name="image",
-    )(place, weights, traces, tx_delay, rx_delay, aperture)
+    )(elem, weights, traces, spots, aperture)
 
 
 BOTH = ("reg", "elem")
@@ -337,16 +342,18 @@
     regions, voxels = rx_delay.shape[0], tx_delay.shape[2]
     devices = n_reg * n_elem
     scale = 8.0 / math.sqrt(n_reg * n_elem * SHIFTS)
-    place = jnp.stack([lax.axis_index("reg"), lax.axis_index("elem")]).astype(jnp.int32)
-    cov, traces = stats(place, rf, tx_delay, rx_delay, aperture)
+    elem = lax.axis_index("elem").astype(jnp.int32).reshape(1)
+    reg = lax.axis_index("reg").astype(jnp.int32).reshape(1)
+    bounds = aperture.T
+    cov, traces, spots = stats(elem, reg, rf, tx_delay, rx_delay, bounds)
     parts = lax.all_to_all(cov, BOTH, 0, 0, tiled=True)
     mine = solve(parts)
     weights = lax.all_to_all(jnp.broadcast_to(mine, (devices, LANES)), BOTH, 0, 0, tiled=True)
-    partial = image(place, weights, traces, tx_delay, rx_delay, aperture)
+    partial = image(scale, elem, weights, traces, spots, bounds)
     owned = partial.reshape(n_reg, regions // n_reg, n_elem, voxels // n_elem).transpose(0, 2, 1, 3)
     owned = owned.reshape(devices, regions // n_reg, voxels // n_elem)
     arrived = lax.all_to_all(owned, BOTH, 0, 0, tiled=True)
-    return jnp.sum(arrived, axis=0) * scale
+    return jnp.sum(arrived, axis=0)
 
 
 def solution(mesh):

time: 136 us -> 101 us (0.74)
  Pallas kernels: 66.4 us -> 38.4 us
  blocking collectives: 60.2 us -> 54.8 us
  local copies, waits for them, and re-layouts: 7.63 us -> 4.38 us
  other arithmetic: 1.38 us -> 2.79 us
    pallas_call x1, Pallas kernels: 56.3 us -> 28.9 us  [stats(): pl.pallas_call(stats_kernel, grid_spec=grid_spec, out_shape=[jax.ShapeDty...]
    all_to_all x1, blocking collectives: 31.6 us -> 26 us  [per_device(): parts = lax.all_to_all(cov, BOTH, 0, 0, tiled=True)]
    all_to_all x0 -> x1, other arithmetic: none -> 2.07 us  [per_device(): parts = lax.all_to_all(cov, BOTH, 0, 0, tiled=True)]
    all_to_all x1, local copies, waits for them, and re-layouts: 2.39 us -> 0.59 us  [per_device(): parts = lax.all_to_all(cov, BOTH, 0, 0, tiled=True)]
    unnamed x12 -> x9, local copies, waits for them, and re-layouts: 4.87 us -> 3.43 us
where the time goes in v2:
time: 101 us; the launch traced here: 100 us
  blocking collectives  54.8 us (54%)
  Pallas kernels  38.4 us (38%)
  local copies, waits for them, and re-layouts  4.38 us (4%)
  other arithmetic  2.79 us (3%)
    pallas_call x1, Pallas kernels, stats(): pl.pallas_call(stats_kernel, grid_spec=grid_spec, out_shape=[jax.ShapeDty...  28.9 us
    all_to_all x1, blocking collectives, per_device(): parts = lax.all_to_all(cov, BOTH, 0, 0, tiled=True)  26 us
    all_to_all x1, blocking collectives, per_device(): arrived = lax.all_to_all(owned, BOTH, 0, 0, tiled=True)  15.2 us
    all_to_all x1, blocking collectives, per_device(): lax.all_to_all(jnp.broadcast_to(mine, (devices, LANES)), BOTH, 0, 0, tile...  13.6 us
    pallas_call x1, Pallas kernels, solve(): pl.pallas_call(solve_kernel, out_shape=jax.ShapeDtypeStruct((1, LANES), j...  6.11 us
    pallas_call x1, Pallas kernels, image(): pl.pallas_call(functools.partial(image_kernel, scale), grid_spec=grid_spe...  3.43 us
    unnamed x9, local copies, waits for them, and re-layouts  3.43 us
    all_to_all x1, other arithmetic, per_device(): parts = lax.all_to_all(cov, BOTH, 0, 0, tiled=True)  2.07 us

profile of v2, /device:TPU:1, one launch (start us, length us, event | category | flops | bytes accessed | tf_op | source)
XLA Modules:
  0.0 100.4 jit_solution(16668736597438388443)
XLA Ops:
  0.0 0.0 copy-start.2
  0.0 28.9 %stats.1 = (bf16[128,2176]{1,0:T(8,128)(2,1)}, bf16[256,2048]{1,0:T(8,128)(2,1)}, s32[128,512]{1,0:T(8,128)}) custom-call(s32[1]{0:T(128)} %bitcast.elem, s32[1]{0:T(128)} %bitcast.1.reg, bf16[1,256,2048]{2,1,0:T(8,128)(2,1)} %rf_ref.1, s32[32,128,512]{2,1,0:T(8,128)} %tx_ref.1, s32[128,256]{1,0:T(8,128)} %rx_ref.1, s32[4,128]{1,0:T(4,128)} %bitcast.14), custom_call_target="tpu_custom_call" | custom-call | tf_op jit(solution)/shard_map/stats/pallas_call | solution.py:203
  28.9 0.6 broadcast.4
  29.5 2.1 %reduce = bf16[128,2176]{1,0:T(8,128)(2,1)S(1)} reduce(bf16[128,1,2176]{2,0,1:T(8,128)(2,1)} %bitcast.18, bf16[]{:T(256)} %broadcast.4), dimensions={1}, to_apply=%copy.9.reduce_sub_computation | reduce | bytes 1114114 | tf_op jit(solution)/shard_map/all_to_all | solution.py:349
  31.5 0.5 reshape.24
  32.1 26.0 %all_to_all.24 = bf16[128,2,1088]{2,1,0:T(2,128)(2,1)S(1)} all-to-all(bf16[128,2,1088]{2,1,0:T(2,128)(2,1)S(1)} %reshape.24), channel_id=1, replica_groups=mesh['elem'=4,'reg'=32] {'reg','elem'}, dimensions={0} | all-to-all | bytes 1114112 | tf_op jit(solution)/shard_map/all_to_all | solution.py:349
  58.1 0.6 reshape.25
  58.7 0.1 copy.14
  58.8 6.1 %solve.1 = f32[1,128]{1,0:T(1,128)S(1)} custom-call(bf16[128,2176]{1,0:T(8,128)(2,1)S(1)} %bitcast.12), custom_call_target="tpu_custom_call" | custom-call | tf_op jit(solution)/shard_map/solve/pallas_call | solution.py:259
  65.0 13.6 %all_to_all.25 = f32[128,1,128]{2,1,0:T(1,128)S(1)} all-to-all(f32[128,1,128]{2,1,0:T(1,128)S(1)} %broadcast_in_dim.2), channel_id=1, replica_groups=mesh['elem'=4,'reg'=32] {'reg','elem'}, dimensions={0} | all-to-all | bytes 131072 | tf_op jit(solution)/shard_map/all_to_all | solution.py:351
  78.5 0.0 copy-done.2
  78.5 0.0 copy-start
  78.5 1.2 %copy-done = bf16[256,2048]{1,0:T(8,128)(2,1)S(1)} copy-done((bf16[256,2048]{1,0:T(8,128)(2,1)S(1)}, bf16[256,2048]{1,0:T(8,128)(2,1)}, u32[]{:S(2)}) %copy-start) | copy-done | bytes 1048600
  79.7 0.0 copy-start.1
  79.7 0.9 copy-done.1
  80.7 3.4 %image.1 = f32[128,512]{1,0:T(8,128)S(1)} custom-call(s32[1]{0:T(128)} %bitcast.elem, f32[128,128]{1,0:T(8,128)S(1)} %bitcast.13, bf16[256,2048]{1,0:T(8,128)(2,1)S(1)} %copy-done, s32[128,512]{1,0:T(8,128)S(1)} %copy-done.1, s32[4,128]{1,0:T(4,128)S(1)} %bitcast.15), custom_call_target="tpu_custom_call" | custom-call | tf_op jit(solution)/shard_map/image/pallas_call | solution.py:327
  84.1 0.1 reshape.22
  84.3 0.2 copy.11
  84.5 15.2 %all_to_all.26 = f32[128,4,128]{2,1,0:T(4,128)S(1)} all-to-all(f32[128,4,128]{2,1,0:T(4,128)S(1)} %copy.11), channel_id=1, replica_groups=mesh['elem'=4,'reg'=32] {'reg','elem'}, dimensions={0} | all-to-all | bytes 524288 | tf_op jit(solution)/shard_map/all_to_all | solution.py:355
  99.7 0.7 reduce_sum.9
  (2 shorter events, 0.1 us)
Async XLA Ops:
  0.0 78.5 %copy-start.2 = (s32[128,4]{0,1:T(4,128)S(1)}, s32[128,4]{0,1:T(4,128)}, u32[]{:S(2)}) copy-start(s32[128,4]{0,1:T(4,128)} %param.7) | copy-start | bytes 6148
  78.5 1.2 %copy-start = (bf16[256,2048]{1,0:T(8,128)(2,1)S(1)}, bf16[256,2048]{1,0:T(8,128)(2,1)}, u32[]{:S(2)}) copy-start(bf16[256,2048]{1,0:T(8,128)(2,1)} %get-tuple-element.9.traces_ref) | copy-start | bytes 3145732
  79.7 0.9 copy-start.1

commit v3 on v2

--- a/solution.py
+++ b/solution.py
@@ -19,7 +19,7 @@
 load_factor = 0.05
 
 DELTAS = (0, 1, 2, 3, 4, -4, -5, -6, -7)
-TILES = 17
+TILES = 18
 WINDOWS = ((1, 0), (-7, 0), (2, 1), (-6, 1), (3, 0), (-5, 0), (3, 1), (-5, 1), (4, 0), (-4, 0), (0, 1))
 
 
@@ -49,9 +49,22 @@
     return high, low
 
 
-def stats_kernel(elem, reg, rf_ref, tx_ref, rx_ref, aperture_ref, cov_ref, traces_ref, spots_ref,
+def stats_kernel(elem, reg, rf_hbm, tx_hbm, rx_hbm, aperture_hbm, cov_ref, traces_ref, spots_ref,
+                 rf_ref, tx_ref, rx_ref, aperture_ref, arrivals,
                  wide, shifted, count32, count16, colmask, rowmask, windows, grams):
-    del reg
+    copies = [
+        pltpu.make_async_copy(source, target, arrivals.at[which])
+        for which, (source, target) in enumerate((
+            (rx_hbm, rx_ref),
+            (aperture_hbm, aperture_ref),
+            (tx_hbm.at[pl.ds(reg[0], 1)], tx_ref),
+            (rf_hbm, rf_ref),
+        ))
+    ]
+    for copy in copies:
+        copy.start()
+    for copy in copies:
+        copy.wait()
     regions = rx_ref.shape[0]
     samples = rf_ref.shape[-1]
     blocks = samples // LANES
@@ -65,7 +78,8 @@
     wide[0:SUB, :] = jnp.zeros((SUB, samples), jnp.float32)
     wide[SUB + WIDTH : 2 * SUB + WIDTH, :] = jnp.zeros((SUB, samples), jnp.float32)
     step = 32
-    for chunk in range(WIDTH // step):
+
+    def trace_rows(chunk):
         rows = slice(chunk * step, (chunk + 1) * step)
         x = rf_ref[0, rows, :].astype(jnp.float32)
         y = tap_weights[0] * pltpu.roll(x, 1, 1)
@@ -89,36 +103,40 @@
                 jnp.where(here, parts[(j + (1 << bit)) % blocks], parts[j]) for j in range(blocks)
             ]
         for j in range(blocks):
-            wide[SUB + chunk * step : SUB + (chunk + 1) * step, j * LANES : (j + 1) * LANES] = parts[j]
+            lanes = slice(j * LANES, (j + 1) * LANES)
+            wide[SUB + chunk * step : SUB + (chunk + 1) * step, lanes] = parts[j]
+            part = parts[j].astype(jnp.bfloat16)
+            shifted[0, rows, lanes] = part
+            traces_ref[rows, lanes] = part
 
     def shift_rows(which, chunk):
-        begin = SUB + DELTAS[which]
-        if isinstance(chunk, int):
-            part = wide[begin + chunk * step : begin + (chunk + 1) * step, :]
-        else:
-            around = wide[pl.ds(pl.multiple_of(chunk * step, step), step + 2 * SUB), :]
-            part = around[begin : begin + step]
-        part = part.astype(jnp.bfloat16)
-        for copy in range(2):
-            shifted[which, pl.ds(pl.multiple_of(copy * WIDTH + chunk * step, step), step), :] = part
-        return part
-
-    for chunk in range(WIDTH // step):
-        traces_ref[chunk * step : (chunk + 1) * step, :] = shift_rows(0, chunk)
-        shift_rows(1, chunk)
+        begin = SUB + DELTAS[which] + chunk * step
+        shifted[which, chunk * step : (chunk + 1) * step, :] = wide[begin : begin + step, :].astype(jnp.bfloat16)
 
     sums = tx_ref[0] + base.astype(jnp.int32)
     spots_ref[...] = sums
     tall = 16
-    high_rows = row_iota((tall, voxels))
-    low_rows = row_iota((LANES, voxels))
-    for r in range(regions):
-        spots = sums[r : r + 1, :]
-        high = jnp.where(spots // LANES == high_rows, 1.0, 0.0).astype(jnp.bfloat16)
-        low = jnp.where((spots & (LANES - 1)) == low_rows, 1.0, 0.0).astype(jnp.bfloat16)
+    packed_rows = row_iota((LANES, voxels)).astype(jnp.float32).astype(jnp.bfloat16)
+    one, zero = jnp.ones((), jnp.bfloat16), jnp.zeros((), jnp.bfloat16)
+    high_spots = (sums // LANES).astype(jnp.float32)
+    low_spots = (sums & (LANES - 1)).astype(jnp.float32)
+
+    def count_region(r):
+        high = jnp.broadcast_to(high_spots[r : r + 1, :], (tall, voxels)).astype(jnp.bfloat16)
+        low = jnp.broadcast_to(low_spots[r : r + 1, :], (tall, voxels)).astype(jnp.bfloat16)
+        low = jnp.concatenate([low] * (LANES // tall), axis=0)
         count32[:, r, :] = lax.dot_general(
-            high, low, (((1,), (1,)), ((), ())), preferred_element_type=jnp.float32
+            jnp.where(high == packed_rows[0:tall], one, zero),
+            jnp.where(low == packed_rows, one, zero),
+            (((1,), (1,)), ((), ())),
+            preferred_element_type=jnp.float32,
         )
+
+    chunks = WIDTH // step
+    for chunk in range(chunks):
+        trace_rows(chunk)
+        for r in range(chunk * regions // chunks, (chunk + 1) * regions // chunks):
+            count_region(r)
     for j in range(blocks):
         count16[j * LANES : (j + 1) * LANES, :] = jnp.transpose(count32[j]).astype(jnp.bfloat16)
 
@@ -142,15 +160,18 @@
     for slot, (delta, half) in enumerate(WINDOWS):
         windows[slot] = window_matrix(delta, half)
 
-    for which, delta in enumerate(DELTAS):
+    def gram_terms(which):
+        delta = DELTAS[which]
         reach = SUB if delta in (1, 2, 3, -5, -6, -7) else SUB // 2 + 1
-        if 1 <= which < len(DELTAS) - 1:
-            for chunk in range(WIDTH // step):
-                shift_rows(which + 1, chunk)
-        lead_rows = shifted[0, 0:WIDTH, :]
-        pairs = [
-            lead_rows * shifted[which, da * PROBE : da * PROBE + WIDTH, :] for da in range(reach)
-        ]
+        if which:
+            for chunk in range(chunks):
+                shift_rows(which, chunk)
+        pairs = []
+        for da in range(reach):
+            cut = WIDTH - da * PROBE
+            pairs.append(shifted[0, 0:cut, :] * shifted[which, WIDTH - cut : WIDTH, :])
+            if da:
+                pairs.append(shifted[0, cut:WIDTH, :] * shifted[which, 0 : WIDTH - cut, :])
         gram = jnp.dot(
             jnp.concatenate(pairs, axis=0), count16[...], preferred_element_type=jnp.float32
         ).astype(jnp.bfloat16)
@@ -161,14 +182,24 @@
         left = jnp.concatenate([windows[WINDOWS.index((delta, half))] for delta, half, da in terms], axis=1)
         right = jnp.concatenate([grams[DELTAS.index(delta), da] for delta, half, da in terms], axis=0)
         out = jnp.dot(left, right, preferred_element_type=jnp.float32)
-        cov_ref[:, tile * LANES : (tile + 1) * LANES] = jnp.transpose(out).astype(cov_ref.dtype)
-
+        lane_at = tile % (TILES // 2) * LANES
+        cov_ref[tile // (TILES // 2), :, lane_at : lane_at + LANES] = jnp.transpose(out).astype(cov_ref.dtype)
+
+    for delta in (1, -7, 2, -6):
+        gram_terms(DELTAS.index(delta))
+    gram_terms(DELTAS.index(3))
     for da in range(SUB):
         put(da, ((1, 0, da), (-7, 0, da), (2, 1, da), (-6, 1, da)))
+    gram_terms(DELTAS.index(-5))
+    gram_terms(DELTAS.index(4))
     for da in range(SUB // 2):
         put(SUB + da, ((3, 0, da), (-5, 0, da), (3, 1, da + 4), (-5, 1, da + 4)))
+    gram_terms(DELTAS.index(-4))
+    gram_terms(DELTAS.index(0))
     for da in range(SUB // 2 + 1):
         put(12 + da, ((4, 0, da), (-4, 0, da), (0, 1, da)))
+    last = (TILES // 2 - 1) * LANES
+    cov_ref[1, :, last:] = jnp.zeros((regions, LANES), cov_ref.dtype)
 
 
 def stats(elem, reg, rf, tx_delay, rx_delay, aperture):
@@ -178,20 +209,20 @@
     grid_spec = pltpu.PrefetchScalarGridSpec(
         num_scalar_prefetch=2,
         grid=(1,),
-        in_specs=[
-            pl.BlockSpec(rf.shape, lambda i, elem, reg: (0, 0, 0)),
-            pl.BlockSpec((1, regions, voxels), lambda i, elem, reg: (reg[0], 0, 0)),
-            pl.BlockSpec(rx_delay.shape, lambda i, elem, reg: (0, 0)),
-            pl.BlockSpec(aperture.shape, lambda i, elem, reg: (0, 0)),
-        ],
+        in_specs=[pl.BlockSpec(memory_space=pltpu.HBM)] * 4,
         out_specs=[
-            pl.BlockSpec((regions, TILES * LANES), lambda i, elem, reg: (0, 0)),
+            pl.BlockSpec((2, regions, TILES // 2 * LANES), lambda i, elem, reg: (0, 0, 0)),
             pl.BlockSpec((WIDTH, samples), lambda i, elem, reg: (0, 0)),
             pl.BlockSpec((regions, voxels), lambda i, elem, reg: (0, 0)),
         ],
         scratch_shapes=[
+            pltpu.VMEM(rf.shape, rf.dtype),
+            pltpu.VMEM((1, regions, voxels), tx_delay.dtype),
+            pltpu.VMEM(rx_delay.shape, rx_delay.dtype),
+            pltpu.VMEM(aperture.shape, aperture.dtype),
+            pltpu.SemaphoreType.DMA((4,)),
             pltpu.VMEM((WIDTH + 2 * SUB, samples), jnp.float32),
-            pltpu.VMEM((len(DELTAS), 2 * WIDTH, samples), jnp.bfloat16),
+            pltpu.VMEM((len(DELTAS), WIDTH, samples), jnp.bfloat16),
             pltpu.VMEM((16, regions, LANES), jnp.float32),
             pltpu.VMEM((samples, regions), jnp.bfloat16),
             pltpu.VMEM((len(DELTAS), WIDTH, regions), jnp.bfloat16),
@@ -204,18 +235,19 @@
         stats_kernel,
         grid_spec=grid_spec,
         out_shape=[
-            jax.ShapeDtypeStruct((regions, TILES * LANES), jnp.bfloat16),
+            jax.ShapeDtypeStruct((2, regions, TILES // 2 * LANES), jnp.bfloat16),
             jax.ShapeDtypeStruct((WIDTH, samples), jnp.bfloat16),
             jax.ShapeDtypeStruct((regions, voxels), jnp.int32),
         ],
-        compiler_params=pltpu.CompilerParams(vmem_limit_bytes=56 * 1024 * 1024),
+        compiler_params=pltpu.CompilerParams(vmem_limit_bytes=44 * 1024 * 1024),
         name="stats",
     )(elem, reg, rf, tx_delay, rx_delay, aperture)
 
 
-def solve_kernel(parts_ref, weights_ref):
-    total = jnp.sum(parts_ref[...].astype(jnp.float32), axis=0, keepdims=True)
-    tiles = [total[:, t * LANES : (t + 1) * LANES] for t in range(TILES)]
+def solve_kernel(total_ref, weights_ref):
+    total = total_ref[...]
+    per = TILES // 2
+    tiles = [total[t // per : t // per + 1, t % per * LANES : (t % per + 1) * LANES] for t in range(TILES)]
     tall = jnp.concatenate(tiles + [jnp.zeros((LANES - TILES, LANES), jnp.float32)], axis=0)
     turned = jnp.transpose(tall)
     table = jnp.concatenate([turned[0:ORDER, 0:ORDER], turned[ORDER:LANES, 0:ORDER]], axis=1)
@@ -243,14 +275,45 @@
     trace = jnp.sum(jnp.sum(jnp.where(diagonal, cov, 0.0), axis=1, keepdims=True), axis=0, keepdims=True)
     cov = cov + jnp.where(diagonal, load_factor * trace / ORDER, 0.0)
     work = jnp.where(lane < ORDER, cov, 1.0)
-    column = i[:, 0:1]
-    for k in range(ORDER):
-        pivot_row = work[k : k + 1, :]
-        inverse = 1.0 / pivot_row[:, k : k + 1]
-        factor = jnp.where(column == k, 0.0, work[:, k : k + 1] * inverse)
-        work = work - factor * pivot_row
-    held = jnp.sum(jnp.where(diagonal, work, 0.0), axis=1, keepdims=True)
-    solved = work[:, ORDER : ORDER + 1] / held
+    high = 8
+    shape = (high, LANES)
+    sublane = row_iota(shape)
+    groups = [work[g : g + high, :] for g in range(0, ORDER, high)]
+    def spread(part, k):
+        return jnp.broadcast_to(part[:, k : k + 1], shape)
+
+    for k in range(0, ORDER, 4):
+        at, inner = k // high, k % high
+        rows = [jnp.broadcast_to(groups[at][inner + n : inner + n + 1, :], shape) for n in range(4)]
+        m = [[spread(rows[n], k + c) for c in range(4)] for n in range(4)]
+        inverse = 1.0 / (m[0][0] * m[1][1] - m[0][1] * m[1][0])
+        i00, i01 = m[1][1] * inverse, -m[0][1] * inverse
+        i10, i11 = -m[1][0] * inverse, m[0][0] * inverse
+        e02, e03 = i00 * m[0][2] + i01 * m[1][2], i00 * m[0][3] + i01 * m[1][3]
+        e12, e13 = i10 * m[0][2] + i11 * m[1][2], i10 * m[0][3] + i11 * m[1][3]
+        first = i00 * rows[0] + i01 * rows[1]
+        second = i10 * rows[0] + i11 * rows[1]
+        third = rows[2] - m[2][0] * first - m[2][1] * second
+        fourth = rows[3] - m[3][0] * first - m[3][1] * second
+        s22 = m[2][2] - m[2][0] * e02 - m[2][1] * e12
+        s23 = m[2][3] - m[2][0] * e03 - m[2][1] * e13
+        s32 = m[3][2] - m[3][0] * e02 - m[3][1] * e12
+        s33 = m[3][3] - m[3][0] * e03 - m[3][1] * e13
+        inverse = 1.0 / (s22 * s33 - s23 * s32)
+        third, fourth = (third * s33 - fourth * s23) * inverse, (fourth * s22 - third * s32) * inverse
+        first = first - e02 * third - e03 * fourth
+        second = second - e12 * third - e13 * fourth
+        solved_rows = (first, second, third, fourth)
+        updated = []
+        for g, part in enumerate(groups):
+            change = sum(spread(part, k + c) * solved_rows[c] for c in range(4))
+            new = part - change
+            if g == at:
+                for c in range(4):
+                    new = jnp.where(sublane == inner + c, solved_rows[c], new)
+            updated.append(new)
+        groups = updated
+    solved = jnp.concatenate(groups, axis=0)[:, ORDER : ORDER + 1]
     row = jnp.sum(jnp.where(diagonal, solved, 0.0), axis=0, keepdims=True)
     weights_ref[...] = row / jnp.sum(row, axis=1, keepdims=True)
 
@@ -277,10 +340,8 @@
     spread = spread.astype(jnp.float32).astype(jnp.bfloat16)
     weights = weights_ref[...]
     high, low = split(weights)
-    rest = (weights - high.astype(jnp.float32) - low.astype(jnp.float32)).astype(jnp.bfloat16)
     gain = jnp.dot(high, spread, preferred_element_type=jnp.float32)
     gain = gain + jnp.dot(low, spread, preferred_element_type=jnp.float32)
-    gain = gain + jnp.dot(rest, spread, preferred_element_type=jnp.float32)
     lane = lane_iota((regions, WIDTH))
     row = lane // PROBE + first_row
     column = lane & (PROBE - 1)
@@ -346,8 +407,8 @@
     reg = lax.axis_index("reg").astype(jnp.int32).reshape(1)
     bounds = aperture.T
     cov, traces, spots = stats(elem, reg, rf, tx_delay, rx_delay, bounds)
-    parts = lax.all_to_all(cov, BOTH, 0, 0, tiled=True)
-    mine = solve(parts)
+    parts = lax.all_to_all(cov.transpose(1, 0, 2), BOTH, 0, 0, tiled=True)
+    mine = solve(jnp.sum(parts.astype(jnp.float32), axis=0))
     weights = lax.all_to_all(jnp.broadcast_to(mine, (devices, LANES)), BOTH, 0, 0, tiled=True)
     partial = image(scale, elem, weights, traces, spots, bounds)
     owned = partial.reshape(n_reg, regions // n_reg, n_elem, voxels // n_elem).transpose(0, 2, 1, 3)

time: 101 us -> 94.7 us (0.938)
  Pallas kernels: 38.4 us -> 34.6 us
  other arithmetic: 2.79 us -> 1.25 us
    pallas_call x1, Pallas kernels: 6.11 us -> 3.48 us  [solve(): pl.pallas_call(solve_kernel, out_shape=jax.ShapeDtypeStruct((1, LANES), j...]
    all_to_all x1 -> x0, other arithmetic: 2.07 us -> none  [per_device(): parts = lax.all_to_all(cov, BOTH, 0, 0, tiled=True)]
    pallas_call x1, Pallas kernels: 28.9 us -> 27.7 us  [stats(): pl.pallas_call(stats_kernel, grid_spec=grid_spec, out_shape=[jax.ShapeDty...]
    unnamed x9 -> x6, local copies, waits for them, and re-layouts: 3.43 us -> 2.81 us
where the time goes in v3:
time: 94.7 us; the launch traced here: 94.4 us
  blocking collectives  54.8 us (58%)
  Pallas kernels  34.6 us (37%)
  local copies, waits for them, and re-layouts  3.78 us (4%)
  other arithmetic  1.25 us (1%)
    pallas_call x1, Pallas kernels, stats(): pl.pallas_call(stats_kernel, grid_spec=grid_spec, out_shape=[jax.ShapeDty...  27.7 us
    all_to_all x1, blocking collectives, per_device(): parts = lax.all_to_all(cov.transpose(1, 0, 2), BOTH, 0, 0, tiled=True)  26 us
    all_to_all x1, blocking collectives, per_device(): arrived = lax.all_to_all(owned, BOTH, 0, 0, tiled=True)  15.2 us
    all_to_all x1, blocking collectives, per_device(): lax.all_to_all(jnp.broadcast_to(mine, (devices, LANES)), BOTH, 0, 0, tile...  13.6 us
    pallas_call x1, Pallas kernels, solve(): pl.pallas_call(solve_kernel, out_shape=jax.ShapeDtypeStruct((1, LANES), j...  3.48 us
    pallas_call x1, Pallas kernels, image(): pl.pallas_call(functools.partial(image_kernel, scale), grid_spec=grid_spe...  3.37 us
    unnamed x6, local copies, waits for them, and re-layouts  2.81 us

profile of v3, /device:TPU:1, one launch (start us, length us, event | category | flops | bytes accessed | tf_op | source)
XLA Modules:
  0.0 94.4 jit_solution(16578724343675401230)
XLA Ops:
  0.0 0.0 copy-start
  0.0 1.2 %copy-done = bf16[1,256,2048]{2,1,0:T(8,128)(2,1)S(1)} copy-done((bf16[1,256,2048]{2,1,0:T(8,128)(2,1)S(1)}, bf16[1,256,2048]{2,1,0:T(8,128)(2,1)}, u32[]{:S(2)}) %copy-start) | copy-done | bytes 1048600
  1.2 0.0 copy-start.1
  1.2 0.9 copy-done.1
  2.1 0.0 copy-start.2
  2.1 0.7 copy-done.2
  2.8 27.7 %stats.1 = (bf16[2,128,1152]{2,1,0:T(8,128)(2,1)S(1)}, bf16[256,2048]{1,0:T(8,128)(2,1)S(1)}, s32[128,512]{1,0:T(8,128)S(1)}) custom-call(s32[1]{0:T(128)} %bitcast.elem, s32[1]{0:T(128)} %bitcast.1.reg, bf16[1,256,2048]{2,1,0:T(8,128)(2,1)S(1)} %copy-done, s32[32,128,512]{2,1,0:T(8,128)} %tx_hbm.1, s32[128,256]{1,0:T(8,128)S(1)} %copy-done.1, ...), custom_call_target="tpu_custom_call" | custom-call | tf_op jit(solution)/shard_map/stats/pallas_call | solution.py:234
  30.6 0.6 copy.6
  31.2 26.0 %all_to_all.18 = bf16[128,2,1152]{2,1,0:T(2,128)(2,1)S(1)} all-to-all(bf16[128,2,1152]{2,1,0:T(2,128)(2,1)S(1)} %copy.6), channel_id=1, replica_groups=mesh['elem'=4,'reg'=32] {'reg','elem'}, dimensions={0} | all-to-all | bytes 1179648 | tf_op jit(solution)/shard_map/all_to_all | solution.py:410
  57.2 0.5 convert_reduce_fusion.total_ref
  57.7 3.5 %solve.1 = f32[1,128]{1,0:T(1,128)S(1)} custom-call(f32[2,1152]{1,0:T(2,128)S(1)} %convert_reduce_fusion.total_ref), custom_call_target="tpu_custom_call" | custom-call | tf_op jit(solution)/shard_map/solve/pallas_call | solution.py:322
  61.2 13.6 %all_to_all.19 = f32[128,1,128]{2,1,0:T(1,128)S(1)} all-to-all(f32[128,1,128]{2,1,0:T(1,128)S(1)} %broadcast_in_dim.2), channel_id=1, replica_groups=mesh['elem'=4,'reg'=32] {'reg','elem'}, dimensions={0} | all-to-all | bytes 131072 | tf_op jit(solution)/shard_map/all_to_all | solution.py:412
  74.8 3.4 %image.1 = f32[128,512]{1,0:T(8,128)S(1)} custom-call(s32[1]{0:T(128)} %bitcast.elem, f32[128,128]{1,0:T(8,128)S(1)} %bitcast.10, bf16[256,2048]{1,0:T(8,128)(2,1)S(1)} %get-tuple-element.9.traces_ref, s32[128,512]{1,0:T(8,128)S(1)} %get-tuple-element.10.spots_ref, s32[4,128]{1,0:T(4,128)S(1)} %bitcast.12), custom_call_target="tpu_custom_call" | custom-call | tf_op jit(solution)/shard_map/image/pallas_call | solution.py:388
  78.1 0.1 reshape.20
  78.3 0.2 copy.8
  78.5 15.2 %all_to_all.20 = f32[128,4,128]{2,1,0:T(4,128)S(1)} all-to-all(f32[128,4,128]{2,1,0:T(4,128)S(1)} %copy.8), channel_id=1, replica_groups=mesh['elem'=4,'reg'=32] {'reg','elem'}, dimensions={0} | all-to-all | bytes 524288 | tf_op jit(solution)/shard_map/all_to_all | solution.py:416
  93.7 0.7 reduce_sum.19
  (2 shorter events, 0.1 us)
Async XLA Ops:
  0.0 1.2 %copy-start = (bf16[1,256,2048]{2,1,0:T(8,128)(2,1)S(1)}, bf16[1,256,2048]{2,1,0:T(8,128)(2,1)}, u32[]{:S(2)}) copy-start(bf16[1,256,2048]{2,1,0:T(8,128)(2,1)} %rf_hbm.1) | copy-start | bytes 3145732
  1.2 0.9 copy-start.1
  2.1 0.7 copy-start.2

commit v4 on v3

--- a/solution.py
+++ b/solution.py
@@ -49,22 +49,12 @@
     return high, low
 
 
-def stats_kernel(elem, reg, rf_hbm, tx_hbm, rx_hbm, aperture_hbm, cov_ref, traces_ref, spots_ref,
-                 rf_ref, tx_ref, rx_ref, aperture_ref, arrivals,
+def stats_kernel(elem, reg, rf_ref, tx_hbm, rx_ref, aperture_ref, keep_ref, send_ref, traces_ref, spots_ref,
+                 tx_ref, arrival,
                  wide, shifted, count32, count16, colmask, rowmask, windows, grams):
-    copies = [
-        pltpu.make_async_copy(source, target, arrivals.at[which])
-        for which, (source, target) in enumerate((
-            (rx_hbm, rx_ref),
-            (aperture_hbm, aperture_ref),
-            (tx_hbm.at[pl.ds(reg[0], 1)], tx_ref),
-            (rf_hbm, rf_ref),
-        ))
-    ]
-    for copy in copies:
-        copy.start()
-    for copy in copies:
-        copy.wait()
+    tx_copy = pltpu.make_async_copy(tx_hbm.at[pl.ds(reg[0], 1)], tx_ref, arrival)
+    tx_copy.start()
+    core = reg[0] & 1
     regions = rx_ref.shape[0]
     samples = rf_ref.shape[-1]
     blocks = samples // LANES
@@ -113,37 +103,51 @@
         begin = SUB + DELTAS[which] + chunk * step
         shifted[which, chunk * step : (chunk + 1) * step, :] = wide[begin : begin + step, :].astype(jnp.bfloat16)
 
+    trace_rows(0)
+    tx_copy.wait()
+
     sums = tx_ref[0] + base.astype(jnp.int32)
     spots_ref[...] = sums
-    tall = 16
-    packed_rows = row_iota((LANES, voxels)).astype(jnp.float32).astype(jnp.bfloat16)
+    tall, fine_bins = 16, 64
+    coarse_bins = samples // fine_bins
+    packed_rows = row_iota((fine_bins, voxels)).astype(jnp.float32).astype(jnp.bfloat16)
     one, zero = jnp.ones((), jnp.bfloat16), jnp.zeros((), jnp.bfloat16)
-    high_spots = (sums // LANES).astype(jnp.float32)
-    low_spots = (sums & (LANES - 1)).astype(jnp.float32)
+    coarse_spots = (sums // fine_bins).astype(jnp.float32)
+    fine_spots = (sums & (fine_bins - 1)).astype(jnp.float32)
+
+    def one_hot(spots, r, bins):
+        line = jnp.broadcast_to(spots[r : r + 1, :], (tall, voxels)).astype(jnp.bfloat16)
+        line = jnp.concatenate([line] * (bins // tall), axis=0)
+        return jnp.where(line == packed_rows[0:bins], one, zero)
 
     def count_region(r):
-        high = jnp.broadcast_to(high_spots[r : r + 1, :], (tall, voxels)).astype(jnp.bfloat16)
-        low = jnp.broadcast_to(low_spots[r : r + 1, :], (tall, voxels)).astype(jnp.bfloat16)
-        low = jnp.concatenate([low] * (LANES // tall), axis=0)
-        count32[:, r, :] = lax.dot_general(
-            jnp.where(high == packed_rows[0:tall], one, zero),
-            jnp.where(low == packed_rows, one, zero),
+        at = (r // 4 % 2 * (regions // 2) + r // 8 * 4 + r % 4) * coarse_bins
+        count32[at : at + coarse_bins, :] = lax.dot_general(
+            one_hot(coarse_spots, r, coarse_bins),
+            one_hot(fine_spots, r, fine_bins),
             (((1,), (1,)), ((), ())),
             preferred_element_type=jnp.float32,
         )
 
     chunks = WIDTH // step
     for chunk in range(chunks):
-        trace_rows(chunk)
+        if chunk:
+            trace_rows(chunk)
         for r in range(chunk * regions // chunks, (chunk + 1) * regions // chunks):
             count_region(r)
     for j in range(blocks):
-        count16[j * LANES : (j + 1) * LANES, :] = jnp.transpose(count32[j]).astype(jnp.bfloat16)
+        both = [count32[pl.ds(2 * j + q, regions, stride=coarse_bins), :] for q in range(2)]
+        count16[j * LANES : (j + 1) * LANES, :] = jnp.transpose(
+            jnp.concatenate(both, axis=1)
+        ).astype(jnp.bfloat16)
 
     element = row_iota((WIDTH, regions))
     row = element // PROBE
     column = element & (PROBE - 1)
-    bounds = aperture_ref[...]
+    place = lane_iota((8, regions))
+    place = place % (regions // 2) // 4 * 8 + place // (regions // 2) * 4 + place % 4
+    bounds = jnp.concatenate([aperture_ref[...], jnp.zeros((4, regions), jnp.int32)], axis=0)
+    bounds = jnp.take_along_axis(bounds, place, axis=1)
     row_lo, row_hi = bounds[0:1, :] - first_row, bounds[1:2, :] - first_row
     col_lo, col_hi = bounds[2:3, :], bounds[3:4, :]
     column_inside = (column >= col_lo) & (column < col_hi)
@@ -182,8 +186,11 @@
         left = jnp.concatenate([windows[WINDOWS.index((delta, half))] for delta, half, da in terms], axis=1)
         right = jnp.concatenate([grams[DELTAS.index(delta), da] for delta, half, da in terms], axis=0)
         out = jnp.dot(left, right, preferred_element_type=jnp.float32)
-        lane_at = tile % (TILES // 2) * LANES
-        cov_ref[tile // (TILES // 2), :, lane_at : lane_at + LANES] = jnp.transpose(out).astype(cov_ref.dtype)
+        out = jnp.transpose(out).astype(jnp.bfloat16)
+        top, bottom = out[: regions // 2], out[regions // 2 :]
+        at = (tile // (TILES // 2), slice(None), pl.ds(tile % (TILES // 2) * LANES, LANES))
+        keep_ref[at] = jnp.where(core == 0, top, bottom)
+        send_ref[at] = jnp.where(core == 0, bottom, top)
 
     for delta in (1, -7, 2, -6):
         gram_terms(DELTAS.index(delta))
@@ -199,45 +206,38 @@
     for da in range(SUB // 2 + 1):
         put(12 + da, ((4, 0, da), (-4, 0, da), (0, 1, da)))
     last = (TILES // 2 - 1) * LANES
-    cov_ref[1, :, last:] = jnp.zeros((regions, LANES), cov_ref.dtype)
+    for ref in (keep_ref, send_ref):
+        ref[1, :, last:] = jnp.zeros((regions // 2, LANES), ref.dtype)
 
 
 def stats(elem, reg, rf, tx_delay, rx_delay, aperture):
     regions = rx_delay.shape[0]
     samples = rf.shape[-1]
     voxels = tx_delay.shape[-1]
-    grid_spec = pltpu.PrefetchScalarGridSpec(
-        num_scalar_prefetch=2,
-        grid=(1,),
-        in_specs=[pl.BlockSpec(memory_space=pltpu.HBM)] * 4,
-        out_specs=[
-            pl.BlockSpec((2, regions, TILES // 2 * LANES), lambda i, elem, reg: (0, 0, 0)),
-            pl.BlockSpec((WIDTH, samples), lambda i, elem, reg: (0, 0)),
-            pl.BlockSpec((regions, voxels), lambda i, elem, reg: (0, 0)),
+    vmem = pl.BlockSpec(memory_space=pltpu.VMEM)
+    smem = pl.BlockSpec(memory_space=pltpu.SMEM)
+    share = jax.ShapeDtypeStruct((2, regions // 2, TILES // 2 * LANES), jnp.bfloat16)
+    return pl.pallas_call(
+        stats_kernel,
+        in_specs=[smem, smem, vmem, pl.BlockSpec(memory_space=pltpu.HBM), vmem, vmem],
+        out_specs=[vmem] * 4,
+        out_shape=[
+            share,
+            share,
+            jax.ShapeDtypeStruct((WIDTH, samples), jnp.bfloat16),
+            jax.ShapeDtypeStruct((regions, voxels), jnp.int32),
         ],
         scratch_shapes=[
-            pltpu.VMEM(rf.shape, rf.dtype),
             pltpu.VMEM((1, regions, voxels), tx_delay.dtype),
-            pltpu.VMEM(rx_delay.shape, rx_delay.dtype),
-            pltpu.VMEM(aperture.shape, aperture.dtype),
-            pltpu.SemaphoreType.DMA((4,)),
+            pltpu.SemaphoreType.DMA,
             pltpu.VMEM((WIDTH + 2 * SUB, samples), jnp.float32),
             pltpu.VMEM((len(DELTAS), WIDTH, samples), jnp.bfloat16),
-            pltpu.VMEM((16, regions, LANES), jnp.float32),
+            pltpu.VMEM((samples // 64 * regions, 64), jnp.float32),
             pltpu.VMEM((samples, regions), jnp.bfloat16),
             pltpu.VMEM((len(DELTAS), WIDTH, regions), jnp.bfloat16),
             pltpu.VMEM((SUB, WIDTH, regions), jnp.bfloat16),
             pltpu.VMEM((len(WINDOWS), LANES, WIDTH), jnp.bfloat16),
             pltpu.VMEM((len(DELTAS), SUB, WIDTH, regions), jnp.bfloat16),
-        ],
-    )
-    return pl.pallas_call(
-        stats_kernel,
-        grid_spec=grid_spec,
-        out_shape=[
-            jax.ShapeDtypeStruct((2, regions, TILES // 2 * LANES), jnp.bfloat16),
-            jax.ShapeDtypeStruct((WIDTH, samples), jnp.bfloat16),
-            jax.ShapeDtypeStruct((regions, voxels), jnp.int32),
         ],
         compiler_params=pltpu.CompilerParams(vmem_limit_bytes=44 * 1024 * 1024),
         name="stats",
@@ -351,9 +351,10 @@
     inside = (row >= bounds[:, 0:1]) & (row < bounds[:, 1:2])
     inside &= (column >= bounds[:, 2:3]) & (column < bounds[:, 3:4])
     high, low = split(jnp.where(inside, gain * scale, 0.0))
-    line_ref[...] = jnp.dot(high, traces_ref[...], preferred_element_type=jnp.float32) + jnp.dot(
-        low, traces_ref[...], preferred_element_type=jnp.float32
+    both = jnp.dot(
+        jnp.concatenate([high, low], axis=0), traces_ref[...], preferred_element_type=jnp.float32
     )
+    line_ref[...] = both[:regions] + both[regions:]
 
     sums = spots_ref[...]
     group = 32
@@ -373,41 +374,36 @@
 def image(scale, elem, weights, traces, spots, aperture):
     regions, voxels = spots.shape
     samples = traces.shape[-1]
-    grid_spec = pltpu.PrefetchScalarGridSpec(
-        num_scalar_prefetch=1,
-        grid=(1,),
-        in_specs=[
-            pl.BlockSpec(weights.shape, lambda i, elem: (0, 0)),
-            pl.BlockSpec(traces.shape, lambda i, elem: (0, 0)),
-            pl.BlockSpec(spots.shape, lambda i, elem: (0, 0)),
-            pl.BlockSpec(aperture.shape, lambda i, elem: (0, 0)),
-        ],
-        out_specs=pl.BlockSpec((regions, voxels), lambda i, elem: (0, 0)),
-        scratch_shapes=[pltpu.VMEM((regions, samples), jnp.float32)],
-    )
+    vmem = pl.BlockSpec(memory_space=pltpu.VMEM)
     return pl.pallas_call(
         functools.partial(image_kernel, scale),
-        grid_spec=grid_spec,
+        in_specs=[pl.BlockSpec(memory_space=pltpu.SMEM), vmem, vmem, vmem, vmem],
+        out_specs=vmem,
         out_shape=jax.ShapeDtypeStruct((regions, voxels), jnp.float32),
+        scratch_shapes=[pltpu.VMEM((regions, samples), jnp.float32)],
         compiler_params=pltpu.CompilerParams(vmem_limit_bytes=32 * 1024 * 1024),
         name="image",
     )(elem, weights, traces, spots, aperture)
 
 
-BOTH = ("reg", "elem")
+REG = ("xy", "core")
+BOTH = ("xy", "core", "elem")
+CHIPS = ("xy", "elem")
 
 
 def per_device(rf, tx_delay, rx_delay, aperture):
-    n_reg = lax.axis_size("reg")
+    n_reg = lax.axis_size("xy") * lax.axis_size("core")
     n_elem = lax.axis_size("elem")
     regions, voxels = rx_delay.shape[0], tx_delay.shape[2]
     devices = n_reg * n_elem
     scale = 8.0 / math.sqrt(n_reg * n_elem * SHIFTS)
     elem = lax.axis_index("elem").astype(jnp.int32).reshape(1)
-    reg = lax.axis_index("reg").astype(jnp.int32).reshape(1)
+    reg = lax.axis_index(REG).astype(jnp.int32).reshape(1)
     bounds = aperture.T
-    cov, traces, spots = stats(elem, reg, rf, tx_delay, rx_delay, bounds)
-    parts = lax.all_to_all(cov.transpose(1, 0, 2), BOTH, 0, 0, tiled=True)
+    keep, send, traces, spots = stats(elem, reg, rf, tx_delay, rx_delay, bounds)
+    other = lax.ppermute(send, "core", [(0, 1), (1, 0)])
+    chip = (keep.astype(jnp.float32) + other.astype(jnp.float32)).astype(jnp.bfloat16)
+    parts = lax.all_to_all(chip.transpose(1, 0, 2), CHIPS, 0, 0, tiled=True)
     mine = solve(jnp.sum(parts.astype(jnp.float32), axis=0))
     weights = lax.all_to_all(jnp.broadcast_to(mine, (devices, LANES)), BOTH, 0, 0, tiled=True)
     partial = image(scale, elem, weights, traces, spots, bounds)
@@ -418,8 +414,10 @@
 
 
 def solution(mesh):
-    in_specs = (P("reg", "elem", None), P(), P(None, "elem"), P())
-    out_specs = P("reg", "elem")
+    n_elem, n_reg = mesh.shape["elem"], mesh.shape["reg"]
+    chips = jax.sharding.Mesh(mesh.devices.reshape(n_elem, n_reg // 2, 2), ("elem", "xy", "core"))
+    in_specs = (P(REG, "elem", None), P(), P(None, "elem"), P())
+    out_specs = P(REG, "elem")
     return jax.shard_map(
-        per_device, mesh=mesh, in_specs=in_specs, out_specs=out_specs, check_vma=False
+        per_device, mesh=chips, in_specs=in_specs, out_specs=out_specs, check_vma=False
     )

time: 94.7 us -> 91.3 us (0.964)
  blocking collectives: 54.8 us -> 51 us
  Pallas kernels: 34.6 us -> 32.7 us
  starting transfers between devices: 0 us -> 1.49 us
  waiting for transfers between devices: 0 us -> 1.21 us
    all_to_all x1, blocking collectives: 26 us -> 20.9 us  [per_device(): parts = lax.all_to_all(chip.transpose(1, 0, 2), CHIPS, 0, 0, tiled=True)]
    pallas_call x2, Pallas kernels: 31.1 us -> 29.2 us  [the longest x1 25.9 us: stats(): pl.pallas_call(stats_kernel, in_specs=[smem, smem, vmem, pl.BlockSpec(mem...]
    ppermute x0 -> x1, starting transfers between devices: none -> 1.49 us  [per_device(): other = lax.ppermute(send, 'core', [(0, 1), (1, 0)])]
    all_to_all x1, blocking collectives: 13.6 us -> 14.9 us  [per_device(): lax.all_to_all(jnp.broadcast_to(mine, (devices, LANES)), BOTH, 0, 0, tile...]
    ppermute x0 -> x1, waiting for transfers between devices: none -> 1.21 us  [per_device(): other = lax.ppermute(send, 'core', [(0, 1), (1, 0)])]
  transfers between devices with their start and end apart: 0 -> 1, of which waited for: 0 -> 1; matrix products, arithmetic and copies ran while one was open for 0% -> 0% of each run, Pallas kernels for 0% -> 0%
where the time goes in v4:
time: 91.3 us; the launch traced here: 91 us
  blocking collectives  51 us (56%)
  Pallas kernels  32.7 us (36%)
  local copies, waits for them, and re-layouts  3.48 us (4%)
  starting transfers between devices  1.49 us (2%)
  waiting for transfers between devices  1.21 us (1%)
  other arithmetic  1.06 us (1%)
    pallas_call x1, Pallas kernels, stats(): pl.pallas_call(stats_kernel, in_specs=[smem, smem, vmem, pl.BlockSpec(mem...  25.9 us
    all_to_all x1, blocking collectives, per_device(): parts = lax.all_to_all(chip.transpose(1, 0, 2), CHIPS, 0, 0, tiled=True)  20.9 us
    all_to_all x1, blocking collectives, per_device(): arrived = lax.all_to_all(owned, BOTH, 0, 0, tiled=True)  15.2 us
    all_to_all x1, blocking collectives, per_device(): lax.all_to_all(jnp.broadcast_to(mine, (devices, LANES)), BOTH, 0, 0, tile...  14.9 us
    pallas_call x1, Pallas kernels, solve(): pl.pallas_call(solve_kernel, out_shape=jax.ShapeDtypeStruct((1, LANES), j...  3.48 us
    pallas_call x1, Pallas kernels, image(): pl.pallas_call(functools.partial(image_kernel, scale), in_specs=[pl.Block...  3.29 us
    unnamed x6, local copies, waits for them, and re-layouts  2.81 us
  transfers between devices with their start and end apart: 1, of which 1 were waited for; matrix products, arithmetic and copies ran while one was open for 0% of the time, Pallas kernels for 0%

profile of v4, /device:TPU:1, one launch (start us, length us, event | category | flops | bytes accessed | tf_op | source)
XLA Modules:
  0.0 91.0 jit_solution(15026997201238839078)
XLA Ops:
  0.0 0.0 copy-start
  0.0 1.2 %copy-done = bf16[1,256,2048]{2,1,0:T(8,128)(2,1)S(1)} copy-done((bf16[1,256,2048]{2,1,0:T(8,128)(2,1)S(1)}, bf16[1,256,2048]{2,1,0:T(8,128)(2,1)}, u32[]{:S(2)}) %copy-start) | copy-done | bytes 1048600
  1.2 0.0 copy-start.1
  1.2 0.9 copy-done.1
  2.1 0.0 copy-start.2
  2.1 0.7 copy-done.2
  2.8 25.9 %stats.1 = (bf16[2,64,1152]{2,1,0:T(8,128)(2,1)S(1)}, bf16[2,64,1152]{2,1,0:T(8,128)(2,1)S(1)}, bf16[256,2048]{1,0:T(8,128)(2,1)S(1)}, s32[128,512]{1,0:T(8,128)S(1)}) custom-call(s32[1]{0:T(128)} %bitcast.elem, s32[1]{0:T(128)} %bitcast.1.reg, bf16[1,256,2048]{2,1,0:T(8,128)(2,1)S(1)} %copy-done, s32[32,128,512]{2,1,0:T(8,128)} %tx_hbm.1, ...), custom_call_target="tpu_custom_call" | custom-call | tf_op jit(solution)/shard_map/stats/pallas_call | solution.py:220
  28.7 1.5 %collective-permute-start = (bf16[2,64,1152]{2,1,0:T(8,128)(2,1)S(1)}, bf16[2,64,1152]{2,1,0:T(8,128)(2,1)S(1)}, u32[]{:S(2)}, u32[]{:S(2)}) collective-permute-start(bf16[2,64,1152]{2,1,0:T(8,128)(2,1)S(1)} %get-tuple-element.10), channel_id=1, source_target_pairs={{0,1},{1,0},{2,3},{3,2},{4,5},{5,4},{6,7},{7,6},{8,9},{9,8},{10,11... | collective-permute-start | bytes 884744 | tf_op jit(solution)/shard_map/ppermute | solution.py:404
  30.2 1.2 %collective-permute-done = bf16[2,64,1152]{2,1,0:T(8,128)(2,1)S(1)} collective-permute-done((bf16[2,64,1152]{2,1,0:T(8,128)(2,1)S(1)}, bf16[2,64,1152]{2,1,0:T(8,128)(2,1)S(1)}, u32[]{:S(2)}, u32[]{:S(2)}) %collective-permute-start) | collective-permute-done | bytes 294944 | tf_op jit(solution)/shard_map/ppermute | solution.py:404
  31.4 0.1 fusion
  31.5 0.3 copy.6
  31.8 20.9 %all_to_all.18 = bf16[64,2,1152]{2,1,0:T(2,128)(2,1)S(1)} all-to-all(bf16[64,2,1152]{2,1,0:T(2,128)(2,1)S(1)} %copy.6), channel_id=1, replica_groups=mesh['elem'=4,'xy'=16,'core'=2] {'xy','elem'}, dimensions={0} | all-to-all | bytes 589824 | tf_op jit(solution)/shard_map/all_to_all | solution.py:406
  52.8 0.3 convert_reduce_fusion.total_ref
  53.0 3.5 %solve.1 = f32[1,128]{1,0:T(1,128)S(1)} custom-call(f32[2,1152]{1,0:T(2,128)S(1)} %convert_reduce_fusion.total_ref), custom_call_target="tpu_custom_call" | custom-call | tf_op jit(solution)/shard_map/solve/pallas_call | solution.py:322
  56.6 14.9 %all_to_all.19 = f32[128,1,128]{2,1,0:T(1,128)S(1)} all-to-all(f32[128,1,128]{2,1,0:T(1,128)S(1)} %broadcast_in_dim.2), channel_id=1, replica_groups=mesh['elem'=4,'xy'=16,'core'=2] {'xy','core','elem'}, dimensions={0} | all-to-all | bytes 131072 | tf_op jit(solution)/shard_map/all_to_all | solution.py:408
  71.4 3.3 %image.1 = f32[128,512]{1,0:T(8,128)S(1)} custom-call(s32[1]{0:T(128)} %bitcast.elem, f32[128,128]{1,0:T(8,128)S(1)} %bitcast.10, bf16[256,2048]{1,0:T(8,128)(2,1)S(1)} %get-tuple-element.11.traces_ref, s32[128,512]{1,0:T(8,128)S(1)} %get-tuple-element.12.spots_ref, s32[4,128]{1,0:T(4,128)S(1)} %bitcast.12), custom_call_target="tpu_custom_call" | custom-call | tf_op jit(solution)/shard_map/image/pallas_call | solution.py:378
  74.7 0.1 reshape.20
  74.9 0.2 copy.8
  75.0 15.2 %all_to_all.20 = f32[128,4,128]{2,1,0:T(4,128)S(1)} all-to-all(f32[128,4,128]{2,1,0:T(4,128)S(1)} %copy.8), channel_id=1, replica_groups=mesh['elem'=4,'xy'=16,'core'=2] {'xy','core','elem'}, dimensions={0} | all-to-all | bytes 524288 | tf_op jit(solution)/shard_map/all_to_all | solution.py:412
  90.3 0.7 reduce_sum.19
  (2 shorter events, 0.1 us)
Async XLA Ops:
  0.0 1.2 %copy-start = (bf16[1,256,2048]{2,1,0:T(8,128)(2,1)S(1)}, bf16[1,256,2048]{2,1,0:T(8,128)(2,1)}, u32[]{:S(2)}) copy-start(bf16[1,256,2048]{2,1,0:T(8,128)(2,1)} %rf_ref.1) | copy-start | bytes 3145732
  1.2 0.9 copy-start.1
  2.1 0.7 copy-start.2
  28.7 2.7 %collective-permute-start = (bf16[2,64,1152]{2,1,0:T(8,128)(2,1)S(1)}, bf16[2,64,1152]{2,1,0:T(8,128)(2,1)S(1)}, u32[]{:S(2)}, u32[]{:S(2)}) collective-permute-start(bf16[2,64,1152]{2,1,0:T(8,128)(2,1)S(1)} %get-tuple-element.10), channel_id=1, source_target_pairs={{0,1},{1,0},{2,3},{3,2},{4,5},{5,4},{6,7},{7,6},{8,9},{9,8},{10,11... | collective-permute-start | bytes 884744 | tf_op jit(solution)/shard_map/ppermute | solution.py:404

commit v5 on v4

--- a/solution.py
+++ b/solution.py
@@ -18,9 +18,12 @@
 tap_weights = (-0.0625, 0.5625, 0.5625, -0.0625)
 load_factor = 0.05
 
-DELTAS = (0, 1, 2, 3, 4, -4, -5, -6, -7)
+DELTAS = (0, 1, 2, 3, 4, -5, -6, -7)
 TILES = 18
-WINDOWS = ((1, 0), (-7, 0), (2, 1), (-6, 1), (3, 0), (-5, 0), (3, 1), (-5, 1), (4, 0), (-4, 0), (0, 1))
+WINDOWS = (
+    (1, 0, 0), (-7, 0, 0), (2, 1, 0), (-6, 1, 0), (3, 0, 0), (-5, 0, 0), (3, 1, 0), (-5, 1, 0),
+    (4, 0, 0), (4, 0, 4), (4, 0, 5), (4, 0, 6), (4, 0, 7), (0, 1, 0), (0, 0, 0),
+)
 
 
 def lane_iota(shape):
@@ -31,13 +34,16 @@
     return lax.broadcasted_iota(jnp.int32, shape, 0)
 
 
-def window_matrix(delta, half):
+def window_matrix(delta, half, turn):
     element = lane_iota((LANES, WIDTH))
     target = row_iota((LANES, WIDTH)) - ORDER * half
     x = target & (SUB - 1)
     k = element & (PROBE - 1)
     good = (target >= 0) & (target < ORDER)
-    good &= (element // PROBE) == (target // SUB)
+    if turn:
+        x = x - 4
+        good &= x >= 0
+    good &= ((element // PROBE + turn) & (SUB - 1)) == (target // SUB)
     good &= (k >= x) & (k <= x + PROBE - SUB)
     good &= (x + delta >= 0) & (x + delta < SUB)
     return good.astype(jnp.float32).astype(jnp.bfloat16)
@@ -161,12 +167,12 @@
         inside = row_inside & (other >= row_lo) & (other < row_hi)
         rowmask[da] = inside.astype(jnp.float32).astype(jnp.bfloat16)
 
-    for slot, (delta, half) in enumerate(WINDOWS):
-        windows[slot] = window_matrix(delta, half)
+    for slot, window in enumerate(WINDOWS):
+        windows[slot] = window_matrix(*window)
 
     def gram_terms(which):
         delta = DELTAS[which]
-        reach = SUB if delta in (1, 2, 3, -5, -6, -7) else SUB // 2 + 1
+        reach = SUB if delta else SUB // 2 + 1
         if which:
             for chunk in range(chunks):
                 shift_rows(which, chunk)
@@ -183,8 +189,8 @@
             grams[which, da] = gram[da * WIDTH : (da + 1) * WIDTH] * colmask[which] * rowmask[da]
 
     def put(tile, terms):
-        left = jnp.concatenate([windows[WINDOWS.index((delta, half))] for delta, half, da in terms], axis=1)
-        right = jnp.concatenate([grams[DELTAS.index(delta), da] for delta, half, da in terms], axis=0)
+        left = jnp.concatenate([windows[WINDOWS.index((delta, half, turn))] for delta, half, turn, da in terms], axis=1)
+        right = jnp.concatenate([grams[DELTAS.index(delta), da] for delta, half, turn, da in terms], axis=0)
         out = jnp.dot(left, right, preferred_element_type=jnp.float32)
         out = jnp.transpose(out).astype(jnp.bfloat16)
         top, bottom = out[: regions // 2], out[regions // 2 :]
@@ -196,15 +202,15 @@
         gram_terms(DELTAS.index(delta))
     gram_terms(DELTAS.index(3))
     for da in range(SUB):
-        put(da, ((1, 0, da), (-7, 0, da), (2, 1, da), (-6, 1, da)))
+        put(da, ((1, 0, 0, da), (-7, 0, 0, da), (2, 1, 0, da), (-6, 1, 0, da)))
     gram_terms(DELTAS.index(-5))
     gram_terms(DELTAS.index(4))
     for da in range(SUB // 2):
-        put(SUB + da, ((3, 0, da), (-5, 0, da), (3, 1, da + 4), (-5, 1, da + 4)))
-    gram_terms(DELTAS.index(-4))
+        put(SUB + da, ((3, 0, 0, da), (-5, 0, 0, da), (3, 1, 0, da + 4), (-5, 1, 0, da + 4)))
     gram_terms(DELTAS.index(0))
-    for da in range(SUB // 2 + 1):
-        put(12 + da, ((4, 0, da), (-4, 0, da), (0, 1, da)))
+    for da in range(SUB // 2):
+        put(12 + da, ((4, 0, 0, da), (4, 0, da + 4, da + 4), (0, 1, 0, da)))
+    put(16, ((0, 0, 0, 4),))
     last = (TILES // 2 - 1) * LANES
     for ref in (keep_ref, send_ref):
         ref[1, :, last:] = jnp.zeros((regions // 2, LANES), ref.dtype)
@@ -256,17 +262,19 @@
     j = lane & (ORDER - 1)
     da = ((j // SUB) - (i // SUB)) & (SUB - 1)
     d = ((j & (SUB - 1)) - (i & (SUB - 1))) & (SUB - 1)
+    low = (i & (SUB - 1)) < 4
     spot = jnp.where(
         d == 1, da,
         jnp.where(
             d == 2, da + ORDER,
             jnp.where(
                 d == 3, SUB + (da & 3) + ORDER * (da // 4),
-                jnp.where(d == 4, 12 + da, 12 + da + ORDER),
+                jnp.where(d == 4, jnp.where(low, 12 + da, 16 - da), jnp.where(da == 4, 16, 12 + da + ORDER)),
             ),
         ),
     )
-    stored = ((d >= 1) & (d <= 3)) | (((d == 0) | (d == 4)) & (da <= 4))
+    stored = ((d >= 1) & (d <= 3)) | ((d == 0) & (da <= 4))
+    stored |= (d == 4) & ((low & (da <= 3)) | (~low & (da >= 1) & (da <= 4)))
     half = jnp.take_along_axis(table, spot & (LANES - 1), axis=1)
     half = jnp.where(stored & (lane < ORDER), half, 0.0)
     square = jnp.concatenate([half, jnp.zeros((LANES - ORDER, LANES), jnp.float32)], axis=0)
@@ -357,21 +365,31 @@
     line_ref[...] = both[:regions] + both[regions:]
 
     sums = spots_ref[...]
+    own = out_ref.shape[2]
     group = 32
+    blocks = samples // LANES
+    near = 9
     for begin in range(0, regions, group):
         rows = slice(begin, begin + group)
+        spots = sums[rows, :]
+        first = jnp.minimum(jnp.min(spots, axis=1, keepdims=True) // LANES, blocks - near)
+        first = jnp.broadcast_to(first, (group, LANES))
+        parts = [line_ref[rows, j * LANES : (j + 1) * LANES] for j in range(blocks)]
+        for bit in (4, 2, 1):
+            here = (first & bit) != 0
+            parts = [jnp.where(here, parts[j + bit], parts[j]) for j in range(near - 1 + bit)]
         for v in range(voxels // LANES):
-            spots = sums[rows, v * LANES : (v + 1) * LANES]
-            fine = spots & (LANES - 1)
-            coarse = spots // LANES
+            spot = spots[:, v * LANES : (v + 1) * LANES]
+            fine = spot & (LANES - 1)
+            coarse = spot // LANES - first
             picked = jnp.zeros((group, LANES), jnp.float32)
-            for j in range(samples // LANES):
-                found = jnp.take_along_axis(line_ref[rows, j * LANES : (j + 1) * LANES], fine, axis=1)
+            for j in range(near):
+                found = jnp.take_along_axis(parts[j], fine, axis=1)
                 picked = jnp.where(coarse == j, found, picked)
-            out_ref[rows, v * LANES : (v + 1) * LANES] = picked
-
-
-def image(scale, elem, weights, traces, spots, aperture):
+            out_ref[begin // own : (begin + group) // own, v] = picked.reshape(group // own, own, LANES)
+
+
+def image(scale, n_reg, elem, weights, traces, spots, aperture):
     regions, voxels = spots.shape
     samples = traces.shape[-1]
     vmem = pl.BlockSpec(memory_space=pltpu.VMEM)
@@ -379,7 +397,7 @@
         functools.partial(image_kernel, scale),
         in_specs=[pl.BlockSpec(memory_space=pltpu.SMEM), vmem, vmem, vmem, vmem],
         out_specs=vmem,
-        out_shape=jax.ShapeDtypeStruct((regions, voxels), jnp.float32),
+        out_shape=jax.ShapeDtypeStruct((n_reg, voxels // LANES, regions // n_reg, LANES), jnp.float32),
         scratch_shapes=[pltpu.VMEM((regions, samples), jnp.float32)],
         compiler_params=pltpu.CompilerParams(vmem_limit_bytes=32 * 1024 * 1024),
         name="image",
@@ -406,9 +424,8 @@
     parts = lax.all_to_all(chip.transpose(1, 0, 2), CHIPS, 0, 0, tiled=True)
     mine = solve(jnp.sum(parts.astype(jnp.float32), axis=0))
     weights = lax.all_to_all(jnp.broadcast_to(mine, (devices, LANES)), BOTH, 0, 0, tiled=True)
-    partial = image(scale, elem, weights, traces, spots, bounds)
-    owned = partial.reshape(n_reg, regions // n_reg, n_elem, voxels // n_elem).transpose(0, 2, 1, 3)
-    owned = owned.reshape(devices, regions // n_reg, voxels // n_elem)
+    partial = image(scale, n_reg, elem, weights, traces, spots, bounds)
+    owned = partial.reshape(devices, regions // n_reg, voxels // n_elem)
     arrived = lax.all_to_all(owned, BOTH, 0, 0, tiled=True)
     return jnp.sum(arrived, axis=0)
 

time: 91.3 us -> 89.5 us (0.980)
  Pallas kernels: 32.7 us -> 31.2 us
where the time goes in v5:
time: 89.5 us; the launch traced here: 89.2 us
  blocking collectives  51 us (57%)
  Pallas kernels  31.2 us (35%)
  local copies, waits for them, and re-layouts  3.16 us (4%)
  starting transfers between devices  1.5 us (2%)
  waiting for transfers between devices  1.21 us (1%)
  other arithmetic  1.06 us (1%)
    pallas_call x1, Pallas kernels, stats(): pl.pallas_call(stats_kernel, in_specs=[smem, smem, vmem, pl.BlockSpec(mem...  25.3 us
    all_to_all x1, blocking collectives, per_device(): parts = lax.all_to_all(chip.transpose(1, 0, 2), CHIPS, 0, 0, tiled=True)  20.9 us
    all_to_all x1, blocking collectives, per_device(): arrived = lax.all_to_all(owned, BOTH, 0, 0, tiled=True)  15.2 us
    all_to_all x1, blocking collectives, per_device(): lax.all_to_all(jnp.broadcast_to(mine, (devices, LANES)), BOTH, 0, 0, tile...  14.9 us
    pallas_call x1, Pallas kernels, solve(): pl.pallas_call(solve_kernel, out_shape=jax.ShapeDtypeStruct((1, LANES), j...  3.48 us
    unnamed x6, local copies, waits for them, and re-layouts  2.81 us
    pallas_call x1, Pallas kernels, image(): pl.pallas_call(functools.partial(image_kernel, scale), in_specs=[pl.Block...  2.44 us
  transfers between devices with their start and end apart: 1, of which 1 were waited for; matrix products, arithmetic and copies ran while one was open for 0% of the time, Pallas kernels for 0%

profile of v5, /device:TPU:1, one launch (start us, length us, event | category | flops | bytes accessed | tf_op | source)
XLA Modules:
  0.0 89.2 jit_solution(1029410932984598607)
XLA Ops:
  0.0 0.0 copy-start
  0.0 1.2 %copy-done = bf16[1,256,2048]{2,1,0:T(8,128)(2,1)S(1)} copy-done((bf16[1,256,2048]{2,1,0:T(8,128)(2,1)S(1)}, bf16[1,256,2048]{2,1,0:T(8,128)(2,1)}, u32[]{:S(2)}) %copy-start) | copy-done | bytes 1048600
  1.2 0.0 copy-start.1
  1.2 0.9 %copy-done.1 = s32[128,256]{1,0:T(8,128)S(1)} copy-done((s32[128,256]{1,0:T(8,128)S(1)}, s32[128,256]{1,0:T(8,128)}, u32[]{:S(2)}) %copy-start.1) | copy-done | bytes 131096
  2.1 0.0 copy-start.2
  2.1 0.7 copy-done.2
  2.8 25.3 %stats.1 = (bf16[2,64,1152]{2,1,0:T(8,128)(2,1)S(1)}, bf16[2,64,1152]{2,1,0:T(8,128)(2,1)S(1)}, bf16[256,2048]{1,0:T(8,128)(2,1)S(1)}, s32[128,512]{1,0:T(8,128)S(1)}) custom-call(s32[1]{0:T(128)} %bitcast.elem, s32[1]{0:T(128)} %bitcast.1.reg, bf16[1,256,2048]{2,1,0:T(8,128)(2,1)S(1)} %copy-done, s32[32,128,512]{2,1,0:T(8,128)} %tx_hbm.1, ...), custom_call_target="tpu_custom_call" | custom-call | tf_op jit(solution)/shard_map/stats/pallas_call | solution.py:226
  28.1 1.5 %collective-permute-start = (bf16[2,64,1152]{2,1,0:T(8,128)(2,1)S(1)}, bf16[2,64,1152]{2,1,0:T(8,128)(2,1)S(1)}, u32[]{:S(2)}, u32[]{:S(2)}) collective-permute-start(bf16[2,64,1152]{2,1,0:T(8,128)(2,1)S(1)} %get-tuple-element.10), channel_id=1, source_target_pairs={{0,1},{1,0},{2,3},{3,2},{4,5},{5,4},{6,7},{7,6},{8,9},{9,8},{10,11... | collective-permute-start | bytes 884744 | tf_op jit(solution)/shard_map/ppermute | solution.py:422
  29.6 1.2 %collective-permute-done = bf16[2,64,1152]{2,1,0:T(8,128)(2,1)S(1)} collective-permute-done((bf16[2,64,1152]{2,1,0:T(8,128)(2,1)S(1)}, bf16[2,64,1152]{2,1,0:T(8,128)(2,1)S(1)}, u32[]{:S(2)}, u32[]{:S(2)}) %collective-permute-start) | collective-permute-done | bytes 294944 | tf_op jit(solution)/shard_map/ppermute | solution.py:422
  30.8 0.1 fusion
  30.9 0.3 copy.5
  31.2 20.9 %all_to_all.18 = bf16[64,2,1152]{2,1,0:T(2,128)(2,1)S(1)} all-to-all(bf16[64,2,1152]{2,1,0:T(2,128)(2,1)S(1)} %copy.5), channel_id=1, replica_groups=mesh['elem'=4,'xy'=16,'core'=2] {'xy','elem'}, dimensions={0} | all-to-all | bytes 589824 | tf_op jit(solution)/shard_map/all_to_all | solution.py:424
  52.1 0.3 convert_reduce_fusion.total_ref
  52.4 3.5 %solve.1 = f32[1,128]{1,0:T(1,128)S(1)} custom-call(f32[2,1152]{1,0:T(2,128)S(1)} %convert_reduce_fusion.total_ref), custom_call_target="tpu_custom_call" | custom-call | tf_op jit(solution)/shard_map/solve/pallas_call | solution.py:330
  56.0 14.9 %all_to_all.19 = f32[128,1,128]{2,1,0:T(1,128)S(1)} all-to-all(f32[128,1,128]{2,1,0:T(1,128)S(1)} %broadcast_in_dim.2), channel_id=1, replica_groups=mesh['elem'=4,'xy'=16,'core'=2] {'xy','core','elem'}, dimensions={0} | all-to-all | bytes 131072 | tf_op jit(solution)/shard_map/all_to_all | solution.py:426
  70.8 2.4 %image.1 = f32[32,4,4,128]{3,2,1,0:T(4,128)S(1)} custom-call(s32[1]{0:T(128)} %bitcast.elem, f32[128,128]{1,0:T(8,128)S(1)} %bitcast.9, bf16[256,2048]{1,0:T(8,128)(2,1)S(1)} %get-tuple-element.11.traces_ref, s32[128,512]{1,0:T(8,128)S(1)} %get-tuple-element.12.spots_ref, s32[4,128]{1,0:T(4,128)S(1)} %bitcast.11), custom_call_target="tpu_custom_call" | custom-call | tf_op jit(solution)/shard_map/image/pallas_call | solution.py:396
  73.3 15.2 %all_to_all.20 = f32[128,4,128]{2,1,0:T(4,128)S(1)} all-to-all(f32[128,4,128]{2,1,0:T(4,128)S(1)} %bitcast.8), channel_id=1, replica_groups=mesh['elem'=4,'xy'=16,'core'=2] {'xy','core','elem'}, dimensions={0} | all-to-all | bytes 524288 | tf_op jit(solution)/shard_map/all_to_all | solution.py:429
  88.5 0.7 reduce_sum.19
  (1 shorter events, 0.0 us)
Async XLA Ops:
  0.0 1.2 %copy-start = (bf16[1,256,2048]{2,1,0:T(8,128)(2,1)S(1)}, bf16[1,256,2048]{2,1,0:T(8,128)(2,1)}, u32[]{:S(2)}) copy-start(bf16[1,256,2048]{2,1,0:T(8,128)(2,1)} %rf_ref.1) | copy-start | bytes 3145732
  1.2 0.9 %copy-start.1 = (s32[128,256]{1,0:T(8,128)S(1)}, s32[128,256]{1,0:T(8,128)}, u32[]{:S(2)}) copy-start(s32[128,256]{1,0:T(8,128)} %rx_ref.1) | copy-start | bytes 393220
  2.1 0.7 copy-start.2
  28.1 2.7 %collective-permute-start = (bf16[2,64,1152]{2,1,0:T(8,128)(2,1)S(1)}, bf16[2,64,1152]{2,1,0:T(8,128)(2,1)S(1)}, u32[]{:S(2)}, u32[]{:S(2)}) collective-permute-start(bf16[2,64,1152]{2,1,0:T(8,128)(2,1)S(1)} %get-tuple-element.10), channel_id=1, source_target_pairs={{0,1},{1,0},{2,3},{3,2},{4,5},{5,4},{6,7},{7,6},{8,9},{9,8},{10,11... | collective-permute-start | bytes 884744 | tf_op jit(solution)/shard_map/ppermute | solution.py:422

commit v6 on v5

--- a/solution.py
+++ b/solution.py
@@ -176,17 +176,20 @@
         if which:
             for chunk in range(chunks):
                 shift_rows(which, chunk)
-        pairs = []
-        for da in range(reach):
-            cut = WIDTH - da * PROBE
-            pairs.append(shifted[0, 0:cut, :] * shifted[which, WIDTH - cut : WIDTH, :])
-            if da:
-                pairs.append(shifted[0, cut:WIDTH, :] * shifted[which, 0 : WIDTH - cut, :])
-        gram = jnp.dot(
-            jnp.concatenate(pairs, axis=0), count16[...], preferred_element_type=jnp.float32
-        ).astype(jnp.bfloat16)
-        for da in range(reach):
-            grams[which, da] = gram[da * WIDTH : (da + 1) * WIDTH] * colmask[which] * rowmask[da]
+        group = 4
+        for begin in range(0, reach, group):
+            held = range(begin, min(begin + group, reach))
+            pairs = []
+            for da in held:
+                cut = WIDTH - da * PROBE
+                pairs.append(shifted[0, 0:cut, :] * shifted[which, WIDTH - cut : WIDTH, :])
+                if da:
+                    pairs.append(shifted[0, cut:WIDTH, :] * shifted[which, 0 : WIDTH - cut, :])
+            gram = jnp.dot(
+                jnp.concatenate(pairs, axis=0), count16[...], preferred_element_type=jnp.float32
+            ).astype(jnp.bfloat16)
+            for n, da in enumerate(held):
+                grams[which, da] = gram[n * WIDTH : (n + 1) * WIDTH] * colmask[which] * rowmask[da]
 
     def put(tile, terms):
         left = jnp.concatenate([windows[WINDOWS.index((delta, half, turn))] for delta, half, turn, da in terms], axis=1)

time: 89.5 us -> 88.3 us (0.987)
  Pallas kernels: 31.2 us -> 30 us
    pallas_call x1, Pallas kernels: 25.3 us -> 24.1 us  [stats(): pl.pallas_call(stats_kernel, in_specs=[smem, smem, vmem, pl.BlockSpec(mem...]
where the time goes in v6:
time: 88.3 us; the launch traced here: 88 us
  blocking collectives  51 us (58%)
  Pallas kernels  30 us (34%)
  local copies, waits for them, and re-layouts  3.16 us (4%)
  starting transfers between devices  1.5 us (2%)
  waiting for transfers between devices  1.21 us (1%)
  other arithmetic  1.06 us (1%)
    pallas_call x1, Pallas kernels, stats(): pl.pallas_call(stats_kernel, in_specs=[smem, smem, vmem, pl.BlockSpec(mem...  24.1 us
    all_to_all x1, blocking collectives, per_device(): parts = lax.all_to_all(chip.transpose(1, 0, 2), CHIPS, 0, 0, tiled=True)  20.9 us
    all_to_all x1, blocking collectives, per_device(): arrived = lax.all_to_all(owned, BOTH, 0, 0, tiled=True)  15.2 us
    all_to_all x1, blocking collectives, per_device(): lax.all_to_all(jnp.broadcast_to(mine, (devices, LANES)), BOTH, 0, 0, tile...  14.9 us
    pallas_call x1, Pallas kernels, solve(): pl.pallas_call(solve_kernel, out_shape=jax.ShapeDtypeStruct((1, LANES), j...  3.48 us
    unnamed x6, local copies, waits for them, and re-layouts  2.81 us
    pallas_call x1, Pallas kernels, image(): pl.pallas_call(functools.partial(image_kernel, scale), in_specs=[pl.Block...  2.44 us
  transfers between devices with their start and end apart: 1, of which 1 were waited for; matrix products, arithmetic and copies ran while one was open for 0% of the time, Pallas kernels for 0%

profile of v6, /device:TPU:1, one launch (start us, length us, event | category | flops | bytes accessed | tf_op | source)
XLA Modules:
  0.0 88.0 jit_solution(11999877524924388382)
XLA Ops:
  0.0 0.0 copy-start
  0.0 1.2 %copy-done = bf16[1,256,2048]{2,1,0:T(8,128)(2,1)S(1)} copy-done((bf16[1,256,2048]{2,1,0:T(8,128)(2,1)S(1)}, bf16[1,256,2048]{2,1,0:T(8,128)(2,1)}, u32[]{:S(2)}) %copy-start) | copy-done | bytes 1048600
  1.2 0.0 copy-start.1
  1.2 0.9 %copy-done.1 = s32[128,256]{1,0:T(8,128)S(1)} copy-done((s32[128,256]{1,0:T(8,128)S(1)}, s32[128,256]{1,0:T(8,128)}, u32[]{:S(2)}) %copy-start.1) | copy-done | bytes 131096
  2.1 0.0 copy-start.2
  2.1 0.7 copy-done.2
  2.8 24.1 %stats.1 = (bf16[2,64,1152]{2,1,0:T(8,128)(2,1)S(1)}, bf16[2,64,1152]{2,1,0:T(8,128)(2,1)S(1)}, bf16[256,2048]{1,0:T(8,128)(2,1)S(1)}, s32[128,512]{1,0:T(8,128)S(1)}) custom-call(s32[1]{0:T(128)} %bitcast.elem, s32[1]{0:T(128)} %bitcast.1.reg, bf16[1,256,2048]{2,1,0:T(8,128)(2,1)S(1)} %copy-done, s32[32,128,512]{2,1,0:T(8,128)} %tx_hbm.1, ...), custom_call_target="tpu_custom_call" | custom-call | tf_op jit(solution)/shard_map/stats/pallas_call | solution.py:229
  26.9 1.5 %collective-permute-start = (bf16[2,64,1152]{2,1,0:T(8,128)(2,1)S(1)}, bf16[2,64,1152]{2,1,0:T(8,128)(2,1)S(1)}, u32[]{:S(2)}, u32[]{:S(2)}) collective-permute-start(bf16[2,64,1152]{2,1,0:T(8,128)(2,1)S(1)} %get-tuple-element.10), channel_id=1, source_target_pairs={{0,1},{1,0},{2,3},{3,2},{4,5},{5,4},{6,7},{7,6},{8,9},{9,8},{10,11... | collective-permute-start | bytes 884744 | tf_op jit(solution)/shard_map/ppermute | solution.py:425
  28.4 1.2 %collective-permute-done = bf16[2,64,1152]{2,1,0:T(8,128)(2,1)S(1)} collective-permute-done((bf16[2,64,1152]{2,1,0:T(8,128)(2,1)S(1)}, bf16[2,64,1152]{2,1,0:T(8,128)(2,1)S(1)}, u32[]{:S(2)}, u32[]{:S(2)}) %collective-permute-start) | collective-permute-done | bytes 294944 | tf_op jit(solution)/shard_map/ppermute | solution.py:425
  29.6 0.1 fusion
  29.7 0.3 copy.5
  30.0 20.9 %all_to_all.18 = bf16[64,2,1152]{2,1,0:T(2,128)(2,1)S(1)} all-to-all(bf16[64,2,1152]{2,1,0:T(2,128)(2,1)S(1)} %copy.5), channel_id=1, replica_groups=mesh['elem'=4,'xy'=16,'core'=2] {'xy','elem'}, dimensions={0} | all-to-all | bytes 589824 | tf_op jit(solution)/shard_map/all_to_all | solution.py:427
  50.9 0.3 convert_reduce_fusion.total_ref
  51.2 3.5 %solve.1 = f32[1,128]{1,0:T(1,128)S(1)} custom-call(f32[2,1152]{1,0:T(2,128)S(1)} %convert_reduce_fusion.total_ref), custom_call_target="tpu_custom_call" | custom-call | tf_op jit(solution)/shard_map/solve/pallas_call | solution.py:333
  54.7 14.9 %all_to_all.19 = f32[128,1,128]{2,1,0:T(1,128)S(1)} all-to-all(f32[128,1,128]{2,1,0:T(1,128)S(1)} %broadcast_in_dim.2), channel_id=1, replica_groups=mesh['elem'=4,'xy'=16,'core'=2] {'xy','core','elem'}, dimensions={0} | all-to-all | bytes 131072 | tf_op jit(solution)/shard_map/all_to_all | solution.py:429
  69.6 2.4 %image.1 = f32[32,4,4,128]{3,2,1,0:T(4,128)S(1)} custom-call(s32[1]{0:T(128)} %bitcast.elem, f32[128,128]{1,0:T(8,128)S(1)} %bitcast.9, bf16[256,2048]{1,0:T(8,128)(2,1)S(1)} %get-tuple-element.11.traces_ref, s32[128,512]{1,0:T(8,128)S(1)} %get-tuple-element.12.spots_ref, s32[4,128]{1,0:T(4,128)S(1)} %bitcast.11), custom_call_target="tpu_custom_call" | custom-call | tf_op jit(solution)/shard_map/image/pallas_call | solution.py:399
  72.0 15.2 %all_to_all.20 = f32[128,4,128]{2,1,0:T(4,128)S(1)} all-to-all(f32[128,4,128]{2,1,0:T(4,128)S(1)} %bitcast.8), channel_id=1, replica_groups=mesh['elem'=4,'xy'=16,'core'=2] {'xy','core','elem'}, dimensions={0} | all-to-all | bytes 524288 | tf_op jit(solution)/shard_map/all_to_all | solution.py:432
  87.3 0.7 reduce_sum.19
  (1 shorter events, 0.0 us)
Async XLA Ops:
  0.0 1.2 %copy-start = (bf16[1,256,2048]{2,1,0:T(8,128)(2,1)S(1)}, bf16[1,256,2048]{2,1,0:T(8,128)(2,1)}, u32[]{:S(2)}) copy-start(bf16[1,256,2048]{2,1,0:T(8,128)(2,1)} %rf_ref.1) | copy-start | bytes 3145732
  1.2 0.9 %copy-start.1 = (s32[128,256]{1,0:T(8,128)S(1)}, s32[128,256]{1,0:T(8,128)}, u32[]{:S(2)}) copy-start(s32[128,256]{1,0:T(8,128)} %rx_ref.1) | copy-start | bytes 393220
  2.1 0.7 copy-start.2
  26.9 2.7 %collective-permute-start = (bf16[2,64,1152]{2,1,0:T(8,128)(2,1)S(1)}, bf16[2,64,1152]{2,1,0:T(8,128)(2,1)S(1)}, u32[]{:S(2)}, u32[]{:S(2)}) collective-permute-start(bf16[2,64,1152]{2,1,0:T(8,128)(2,1)S(1)} %get-tuple-element.10), channel_id=1, source_target_pairs={{0,1},{1,0},{2,3},{3,2},{4,5},{5,4},{6,7},{7,6},{8,9},{9,8},{10,11... | collective-permute-start | bytes 884744 | tf_op jit(solution)/shard_map/ppermute | solution.py:425

commit v7 on v6

--- a/solution.py
+++ b/solution.py
@@ -167,8 +167,6 @@
         inside = row_inside & (other >= row_lo) & (other < row_hi)
         rowmask[da] = inside.astype(jnp.float32).astype(jnp.bfloat16)
 
-    for slot, window in enumerate(WINDOWS):
-        windows[slot] = window_matrix(*window)
 
     def gram_terms(which):
         delta = DELTAS[which]
@@ -201,8 +199,10 @@
         keep_ref[at] = jnp.where(core == 0, top, bottom)
         send_ref[at] = jnp.where(core == 0, bottom, top)
 
-    for delta in (1, -7, 2, -6):
+    for n, delta in enumerate((1, -7, 2, -6)):
         gram_terms(DELTAS.index(delta))
+        for slot in range(4 * n, min(4 * n + 4, len(WINDOWS))):
+            windows[slot] = window_matrix(*WINDOWS[slot])
     gram_terms(DELTAS.index(3))
     for da in range(SUB):
         put(da, ((1, 0, 0, da), (-7, 0, 0, da), (2, 1, 0, da), (-6, 1, 0, da)))

time: 88.3 us -> 88.3 us (level)
  no operation moved by 1% of the time
where the time goes in v7:
time: 88.3 us; the launch traced here: 88 us
  blocking collectives  51 us (58%)
  Pallas kernels  30 us (34%)
  local copies, waits for them, and re-layouts  3.16 us (4%)
  starting transfers between devices  1.5 us (2%)
  waiting for transfers between devices  1.21 us (1%)
  other arithmetic  1.06 us (1%)
    pallas_call x1, Pallas kernels, stats(): pl.pallas_call(stats_kernel, in_specs=[smem, smem, vmem, pl.BlockSpec(mem...  24.1 us
    all_to_all x1, blocking collectives, per_device(): parts = lax.all_to_all(chip.transpose(1, 0, 2), CHIPS, 0, 0, tiled=True)  20.9 us
    all_to_all x1, blocking collectives, per_device(): arrived = lax.all_to_all(owned, BOTH, 0, 0, tiled=True)  15.2 us
    all_to_all x1, blocking collectives, per_device(): lax.all_to_all(jnp.broadcast_to(mine, (devices, LANES)), BOTH, 0, 0, tile...  14.9 us
    pallas_call x1, Pallas kernels, solve(): pl.pallas_call(solve_kernel, out_shape=jax.ShapeDtypeStruct((1, LANES), j...  3.48 us
    unnamed x6, local copies, waits for them, and re-layouts  2.81 us
    pallas_call x1, Pallas kernels, image(): pl.pallas_call(functools.partial(image_kernel, scale), in_specs=[pl.Block...  2.44 us
  transfers between devices with their start and end apart: 1, of which 1 were waited for; matrix products, arithmetic and copies ran while one was open for 0% of the time, Pallas kernels for 0%

profile of v7, /device:TPU:1, one launch (start us, length us, event | category | flops | bytes accessed | tf_op | source)
XLA Modules:
  0.0 88.0 jit_solution(11999877524924388382)
XLA Ops:
  0.0 0.0 copy-start
  0.0 1.2 %copy-done = bf16[1,256,2048]{2,1,0:T(8,128)(2,1)S(1)} copy-done((bf16[1,256,2048]{2,1,0:T(8,128)(2,1)S(1)}, bf16[1,256,2048]{2,1,0:T(8,128)(2,1)}, u32[]{:S(2)}) %copy-start) | copy-done | bytes 1048600
  1.2 0.0 copy-start.1
  1.2 0.9 %copy-done.1 = s32[128,256]{1,0:T(8,128)S(1)} copy-done((s32[128,256]{1,0:T(8,128)S(1)}, s32[128,256]{1,0:T(8,128)}, u32[]{:S(2)}) %copy-start.1) | copy-done | bytes 131096
  2.1 0.0 copy-start.2
  2.1 0.7 copy-done.2
  2.8 24.1 %stats.1 = (bf16[2,64,1152]{2,1,0:T(8,128)(2,1)S(1)}, bf16[2,64,1152]{2,1,0:T(8,128)(2,1)S(1)}, bf16[256,2048]{1,0:T(8,128)(2,1)S(1)}, s32[128,512]{1,0:T(8,128)S(1)}) custom-call(s32[1]{0:T(128)} %bitcast.elem, s32[1]{0:T(128)} %bitcast.1.reg, bf16[1,256,2048]{2,1,0:T(8,128)(2,1)S(1)} %copy-done, s32[32,128,512]{2,1,0:T(8,128)} %tx_hbm.1, ...), custom_call_target="tpu_custom_call" | custom-call | tf_op jit(solution)/shard_map/stats/pallas_call | solution.py:229
  26.9 1.5 %collective-permute-start = (bf16[2,64,1152]{2,1,0:T(8,128)(2,1)S(1)}, bf16[2,64,1152]{2,1,0:T(8,128)(2,1)S(1)}, u32[]{:S(2)}, u32[]{:S(2)}) collective-permute-start(bf16[2,64,1152]{2,1,0:T(8,128)(2,1)S(1)} %get-tuple-element.10), channel_id=1, source_target_pairs={{0,1},{1,0},{2,3},{3,2},{4,5},{5,4},{6,7},{7,6},{8,9},{9,8},{10,11... | collective-permute-start | bytes 884744 | tf_op jit(solution)/shard_map/ppermute | solution.py:425
  28.4 1.2 %collective-permute-done = bf16[2,64,1152]{2,1,0:T(8,128)(2,1)S(1)} collective-permute-done((bf16[2,64,1152]{2,1,0:T(8,128)(2,1)S(1)}, bf16[2,64,1152]{2,1,0:T(8,128)(2,1)S(1)}, u32[]{:S(2)}, u32[]{:S(2)}) %collective-permute-start) | collective-permute-done | bytes 294944 | tf_op jit(solution)/shard_map/ppermute | solution.py:425
  29.6 0.1 fusion
  29.7 0.3 copy.5
  30.0 20.9 %all_to_all.18 = bf16[64,2,1152]{2,1,0:T(2,128)(2,1)S(1)} all-to-all(bf16[64,2,1152]{2,1,0:T(2,128)(2,1)S(1)} %copy.5), channel_id=1, replica_groups=mesh['elem'=4,'xy'=16,'core'=2] {'xy','elem'}, dimensions={0} | all-to-all | bytes 589824 | tf_op jit(solution)/shard_map/all_to_all | solution.py:427
  50.9 0.3 convert_reduce_fusion.total_ref
  51.2 3.5 %solve.1 = f32[1,128]{1,0:T(1,128)S(1)} custom-call(f32[2,1152]{1,0:T(2,128)S(1)} %convert_reduce_fusion.total_ref), custom_call_target="tpu_custom_call" | custom-call | tf_op jit(solution)/shard_map/solve/pallas_call | solution.py:333
  54.7 14.9 %all_to_all.19 = f32[128,1,128]{2,1,0:T(1,128)S(1)} all-to-all(f32[128,1,128]{2,1,0:T(1,128)S(1)} %broadcast_in_dim.2), channel_id=1, replica_groups=mesh['elem'=4,'xy'=16,'core'=2] {'xy','core','elem'}, dimensions={0} | all-to-all | bytes 131072 | tf_op jit(solution)/shard_map/all_to_all | solution.py:429
  69.6 2.4 %image.1 = f32[32,4,4,128]{3,2,1,0:T(4,128)S(1)} custom-call(s32[1]{0:T(128)} %bitcast.elem, f32[128,128]{1,0:T(8,128)S(1)} %bitcast.9, bf16[256,2048]{1,0:T(8,128)(2,1)S(1)} %get-tuple-element.11.traces_ref, s32[128,512]{1,0:T(8,128)S(1)} %get-tuple-element.12.spots_ref, s32[4,128]{1,0:T(4,128)S(1)} %bitcast.11), custom_call_target="tpu_custom_call" | custom-call | tf_op jit(solution)/shard_map/image/pallas_call | solution.py:399
  72.0 15.2 %all_to_all.20 = f32[128,4,128]{2,1,0:T(4,128)S(1)} all-to-all(f32[128,4,128]{2,1,0:T(4,128)S(1)} %bitcast.8), channel_id=1, replica_groups=mesh['elem'=4,'xy'=16,'core'=2] {'xy','core','elem'}, dimensions={0} | all-to-all | bytes 524288 | tf_op jit(solution)/shard_map/all_to_all | solution.py:432
  87.3 0.7 reduce_sum.19
  (1 shorter events, 0.0 us)
Async XLA Ops:
  0.0 1.2 %copy-start = (bf16[1,256,2048]{2,1,0:T(8,128)(2,1)S(1)}, bf16[1,256,2048]{2,1,0:T(8,128)(2,1)}, u32[]{:S(2)}) copy-start(bf16[1,256,2048]{2,1,0:T(8,128)(2,1)} %rf_ref.1) | copy-start | bytes 3145732
  1.2 0.9 %copy-start.1 = (s32[128,256]{1,0:T(8,128)S(1)}, s32[128,256]{1,0:T(8,128)}, u32[]{:S(2)}) copy-start(s32[128,256]{1,0:T(8,128)} %rx_ref.1) | copy-start | bytes 393220
  2.1 0.7 copy-start.2
  26.9 2.7 %collective-permute-start = (bf16[2,64,1152]{2,1,0:T(8,128)(2,1)S(1)}, bf16[2,64,1152]{2,1,0:T(8,128)(2,1)S(1)}, u32[]{:S(2)}, u32[]{:S(2)}) collective-permute-start(bf16[2,64,1152]{2,1,0:T(8,128)(2,1)S(1)} %get-tuple-element.10), channel_id=1, source_target_pairs={{0,1},{1,0},{2,3},{3,2},{4,5},{5,4},{6,7},{7,6},{8,9},{9,8},{10,11... | collective-permute-start | bytes 884744 | tf_op jit(solution)/shard_map/ppermute | solution.py:425
